TPU v7x, 32 devices: a whole 2x2x4 slice. The times are simulated.
32 devices in a mesh: ens: 2 (over y), mom: 8 (over z, x), src: 2 (over core).
Axes of the slice: x: 2, y: 2, z: 4, core: 2. Of those that a mesh axis runs over, the one named last changes fastest.
Arguments:
- fields: bfloat16 [16, 8, 2, 6, 2, 128, 128], P(('ens', 'mom'), 'src'), parts along dimension 0, may hold values from -0.29882812 to 0.29882812
- block_cols: int32 [16, 8, 6, 2], P(('ens', 'mom'), 'src'), parts along dimension 0, may hold values from 0 to 5, as said below
- sources: int32 [2], P('src'), may hold values from 0 to 7, as said below
- deltas: int32 [4], replicated, may hold values from 1 to 7
- partner: int32 [8], P('mom'), may hold values from 0 to 7, as said below
Outputs:
- correlator: float32 [2, 4, 16], P(None, 'src', ('ens', 'mom')), parts along dimension 2
There are 2 independent parts, one for each index of `ens`. A program takes and returns all parts, laid end to end along the dimension named above; an argument that names none is the same for every part. Nothing has to cross between parts.
Inputs may be any that keep to these rules, and one draw needn't show every extreme that they name: `block_cols`: within each block row of each field the 2 block columns are distinct. `sources`: entry s lies among the timeslices s * 4 to (s + 1) * 4 - 1. partner is an involution without fixed points. Momenta g * 1 to (g + 1) - 1 form group g; the partners of group g's momenta are the momenta of group g XOR (8 / 2).
All inputs are finite; a program needn't handle non-finite values.
Results may differ from a plain program's by a relative error of at most 0.0095.
Values may be sent and summed in bfloat16 or wider, within the bound.
No kernel may reach another device: no remote copies, remote signals or barrier semaphores. Data moves between devices by JAX's collectives and lax.ppermute only.
A program may use at most 128 MiB of HBM per device.

v0:
```python
import jax
import jax.numpy as jnp
from jax import lax
from jax.sharding import PartitionSpec as P


def from_partner(value, axis, stride):
    mask = 2**stride
    pairs = [(source, source ^ mask) for source in range(lax.axis_size(axis))]
    return lax.ppermute(value, axis, pairs)


def block_product(left, left_cols, right, right_cols):
    row_blocks = left.shape[1]
    per_row = left.shape[2]
    block_size = left.shape[3]
    flat_cols = left_cols.reshape(-1).astype(jnp.int32)
    picked = jnp.take(right, flat_cols, axis=1).reshape(
        2, row_blocks, per_row, per_row, block_size, block_size
    )
    target = jnp.take(right_cols, flat_cols, axis=0).reshape(row_blocks, per_row, per_row)
    real_part = jnp.einsum(
        "rjab,rjkbe->rjkae", left[0], picked[0], preferred_element_type=jnp.float32
    ) - jnp.einsum("rjab,rjkbe->rjkae", left[1], picked[1], preferred_element_type=jnp.float32)
    imag_part = jnp.einsum(
        "rjab,rjkbe->rjkae", left[0], picked[1], preferred_element_type=jnp.float32
    ) + jnp.einsum("rjab,rjkbe->rjkae", left[1], picked[0], preferred_element_type=jnp.float32)
    onehot = (target[..., None] == jnp.arange(row_blocks, dtype=jnp.int32)).astype(jnp.float32)
    stacked = jnp.stack([real_part, imag_part])
    combined = jnp.einsum("rjkc,xrjkae->xrace", onehot, stacked, precision=lax.Precision.HIGHEST)
    return combined.reshape(2, row_blocks * block_size, row_blocks * block_size).astype(
        jnp.bfloat16
    )


def pair_term(first, second):
    first_wide = first.astype(jnp.float32)
    second_wide = second.astype(jnp.float32)
    trace_first = jnp.trace(first_wide, axis1=1, axis2=2)
    trace_second = jnp.trace(second_wide, axis1=1, axis2=2)
    direct_real = trace_first[0] * trace_second[0] - trace_first[1] * trace_second[1]
    direct_imag = trace_first[0] * trace_second[1] + trace_first[1] * trace_second[0]
    second_flip = jnp.swapaxes(second_wide, 1, 2)
    cross_real = jnp.sum(first_wide[0] * second_flip[0] - first_wide[1] * second_flip[1])
    cross_imag = jnp.sum(first_wide[0] * second_flip[1] + first_wide[1] * second_flip[0])
    return jnp.stack([direct_real - cross_real, direct_imag - cross_imag])


def local(fields, block_cols, sources, deltas, partner):
    slot_count = fields.shape[0]
    local_times = fields.shape[1]
    delta_count = deltas.shape[0]
    total_times = local_times * lax.axis_size("src")
    top_bit = lax.axis_size("mom").bit_length() - 2
    source_time = sources[0]
    sink_times = (source_time + deltas) % total_times
    mirror_slots = partner % slot_count
    far_fields, far_cols = from_partner((fields, block_cols), "mom", top_bit)
    own_all, own_cols, mirror_set, mirror_cols = (
        lax.all_gather(fields, "src", axis=1, tiled=True),
        lax.all_gather(block_cols, "src", axis=1, tiled=True),
        lax.all_gather(far_fields, "src", axis=1, tiled=True),
        lax.all_gather(far_cols, "src", axis=1, tiled=True),
    )

    def one_item(item_index):
        row_slot = item_index // delta_count
        delta_row = item_index % delta_count
        mirror_slot = mirror_slots[row_slot]
        sink_time = sink_times[delta_row]
        mirror_sink = sink_times[delta_row]
        first = block_product(
            own_all[row_slot, source_time],
            own_cols[row_slot, source_time],
            mirror_set[mirror_slot, mirror_sink],
            mirror_cols[mirror_slot, mirror_sink],
        )
        second = block_product(
            mirror_set[mirror_slot, source_time],
            mirror_cols[mirror_slot, source_time],
            own_all[row_slot, sink_time],
            own_cols[row_slot, sink_time],
        )
        return pair_term(first, second)

    results = lax.map(one_item, jnp.arange(slot_count * delta_count, dtype=jnp.int32))
    partial_terms = jnp.transpose(results.reshape(slot_count, delta_count, 2), (2, 1, 0))
    return lax.psum_scatter(partial_terms, "src", scatter_dimension=1, tiled=True)


def solution(mesh):
    in_specs = (
        P(("ens", "mom"), "src", None, None, None, None, None),
        P(("ens", "mom"), "src", None, None),
        P("src"),
        P(),
        P("mom"),
    )
    out_specs = P(None, "src", ("ens", "mom"))
    return jax.shard_map(local, mesh=mesh, in_specs=in_specs, out_specs=out_specs, check_vma=False)
```

profile of v0, /device:TPU:8, one launch (start us, length us, event | category | flops | bytes accessed | tf_op | source)
XLA Modules:
  0.0 511.8 jit_solution(7603544450409978224)
XLA Ops:
  8.4 2.6 collective-permute-start
  11.0 134.7 %collective-permute-done = bf16[1,4,2,6,2,128,128]{6,5,4,3,2,0,1:T(8,128)(2,1)} collective-permute-done((bf16[1,4,2,6,2,128,128]{6,5,4,3,2,0,1:T(8,128)(2,1)S(1)}, bf16[1,4,2,6,2,128,128]{6,5,4,3,2,0,1:T(8,128)(2,1)}, u32[]{:S(2)}, u32[]{:S(2)}) %collective-permute-start) | collective-permute-done | bytes 3145760 | tf_op jit(solution)/shard_map/ppermute | solution.py:10
  145.7 3.6 collective-permute-start.1
  155.2 2.2 dynamic-slice_bitcast_fusion.5
  157.4 7.5 %all-gather.3.cloned.1.call-done = bf16[1,8,2,6,2,128,128]{6,5,4,3,2,0,1:T(8,128)(2,1)} async-done(((bf16[1,4,2,6,2,128,128]{6,5,4,3,2,0,1:T(8,128)(2,1)}), bf16[1,8,2,6,2,128,128]{6,5,4,3,2,0,1:T(8,128)(2,1)}) %all-gather.3.cloned.1.call-update) | async-done | bytes 6291472 | tf_op jit(solution)/shard_map/all_gather | solution.py:62
  164.9 2.1 dynamic-slice_bitcast_fusion.4
  167.0 334.7 %while.14 = (s32[]{:T(128)}, f32[4,2]{1,0:T(4,128)S(1)}, s32[4]{0:T(128)S(1)}, s32[4]{0:T(128)S(1)}, bf16[1,8,2,6,2,128,128]{6,5,4,3,2,1,0:T(8,128)(2,1)}, /*ind...) while((s32[]{:T(128)}, f32[4,2]{1,0:T(4,128)S(1)}, ...), condition=%wide.wide.region_5.8_spmd, body=%wide.wide.region_0.7_spmd.sunk | while | flops 938020864 | bytes 168707120 | solution.py:86
  174.1 2.2 broadcast_compare_fusion.3
  185.8 4.5 copy.89
  196.0 5.8 %copy.87 = f32[2,6,2,2,128,128]{5,3,2,4,0,1:T(2,128)} copy(f32[2,6,2,2,128,128]{4,5,3,2,1,0:T(8,128)} %pad_maximum_fusion.6) | data formatting | bytes 6291456 | tf_op jit(solution)/shard_map/while/body/eval_jaxpr/stack | solution.py:29
  201.7 7.6 %convert_bitcast_fusion.4 = f32[2,6,128,6,128]{4,3,2,0,1:T(8,128)S(1)} fusion(f32[2,6,2,2,128,128]{5,3,2,4,0,1:T(2,128)} %copy.87, s32[6,2,2]{2,1,0:T(2,128)S(1)} %reshape.182), kind=kOutput, calls=%fused_computation.7.clone.clone.1 | convolution fusion | flops 58982544 | bytes 7864416 | tf_op jit(solution)/shard_map/while/body/eval_jaxpr/rjkc,xrjkae->xrace/dot_general | solution.py:30
  209.3 8.6 %select_reduce_fusion.4 = (f32[2]{0:T(128)S(1)}, f32[2]{0:T(128)S(1)}, f32[2,6,128,6,128]{4,3,2,0,1:T(8,128)}) fusion(pred[6,128,6,128]{3,2,1,0:T(8,128)(4,1)S(1)} %copy-done.3, f32[2,6,128,6,128]{4,3,2,0,1:T(8,128)S(1)} %convert_bitcast_fusion.4, f32[2,6,2,2,128,128]{5,3,2,4,0,1:T(2,128)S(1)} %copy.89, s32[6,2,2]{2,1,0:T(2,128)S(1)} %reshape.183), kind=kOutput, calls=%fused_computation.8.clone.clone.1 | convolution fusion | flops 63701132 | bytes 13172848 | tf_op jit(solution)/shard_map/while/body/eval_jaxpr/rjkc,xrjkae->xrace/dot_general | solution.py:30
  218.0 2.1 fusion.127
  220.1 4.2 slice.280
  232.5 5.4 %copy.91 = f32[2,6,128,6,128]{2,1,4,3,0:T(8,128)} copy(f32[2,6,128,6,128]{4,3,2,0,1:T(8,128)} %get-tuple-element.449) | data formatting | bytes 9437184 | tf_op jit(solution)/shard_map/while/body/eval_jaxpr/transpose | solution.py:43
  237.9 7.0 %reshape.184 = f32[2,768,768]{1,2,0:T(8,128)} reshape(f32[2,6,128,6,128]{2,1,4,3,0:T(8,128)} %copy.91) | data formatting | bytes 9437184 | tf_op jit(solution)/shard_map/while/body/eval_jaxpr/transpose | solution.py:43
  244.9 4.4 subtract_reduce_fusion.3
  257.8 2.2 broadcast_compare_fusion.3
  269.5 4.5 copy.89
  279.7 5.8 %copy.87 = f32[2,6,2,2,128,128]{5,3,2,4,0,1:T(2,128)} copy(f32[2,6,2,2,128,128]{4,5,3,2,1,0:T(8,128)} %pad_maximum_fusion.6) | data formatting | bytes 6291456 | tf_op jit(solution)/shard_map/while/body/eval_jaxpr/stack | solution.py:29
  285.4 7.6 %convert_bitcast_fusion.4 = f32[2,6,128,6,128]{4,3,2,0,1:T(8,128)S(1)} fusion(f32[2,6,2,2,128,128]{5,3,2,4,0,1:T(2,128)} %copy.87, s32[6,2,2]{2,1,0:T(2,128)S(1)} %reshape.182), kind=kOutput, calls=%fused_computation.7.clone.clone.1 | convolution fusion | flops 58982544 | bytes 7864416 | tf_op jit(solution)/shard_map/while/body/eval_jaxpr/rjkc,xrjkae->xrace/dot_general | solution.py:30
  293.0 8.6 %select_reduce_fusion.4 = (f32[2]{0:T(128)S(1)}, f32[2]{0:T(128)S(1)}, f32[2,6,128,6,128]{4,3,2,0,1:T(8,128)}) fusion(pred[6,128,6,128]{3,2,1,0:T(8,128)(4,1)S(1)} %copy-done.3, f32[2,6,128,6,128]{4,3,2,0,1:T(8,128)S(1)} %convert_bitcast_fusion.4, f32[2,6,2,2,128,128]{5,3,2,4,0,1:T(2,128)S(1)} %copy.89, s32[6,2,2]{2,1,0:T(2,128)S(1)} %reshape.183), kind=kOutput, calls=%fused_computation.8.clone.clone.1 | convolution fusion | flops 63701132 | bytes 13172848 | tf_op jit(solution)/shard_map/while/body/eval_jaxpr/rjkc,xrjkae->xrace/dot_general | solution.py:30
  301.7 2.1 fusion.127
  303.8 4.2 slice.280
  316.2 5.4 %copy.91 = f32[2,6,128,6,128]{2,1,4,3,0:T(8,128)} copy(f32[2,6,128,6,128]{4,3,2,0,1:T(8,128)} %get-tuple-element.449) | data formatting | bytes 9437184 | tf_op jit(solution)/shard_map/while/body/eval_jaxpr/transpose | solution.py:43
  321.6 7.0 %reshape.184 = f32[2,768,768]{1,2,0:T(8,128)} reshape(f32[2,6,128,6,128]{2,1,4,3,0:T(8,128)} %copy.91) | data formatting | bytes 9437184 | tf_op jit(solution)/shard_map/while/body/eval_jaxpr/transpose | solution.py:43
  328.6 4.4 subtract_reduce_fusion.3
  341.4 2.2 broadcast_compare_fusion.3
  353.2 4.5 copy.89
  363.3 5.8 %copy.87 = f32[2,6,2,2,128,128]{5,3,2,4,0,1:T(2,128)} copy(f32[2,6,2,2,128,128]{4,5,3,2,1,0:T(8,128)} %pad_maximum_fusion.6) | data formatting | bytes 6291456 | tf_op jit(solution)/shard_map/while/body/eval_jaxpr/stack | solution.py:29
  369.1 7.6 %convert_bitcast_fusion.4 = f32[2,6,128,6,128]{4,3,2,0,1:T(8,128)S(1)} fusion(f32[2,6,2,2,128,128]{5,3,2,4,0,1:T(2,128)} %copy.87, s32[6,2,2]{2,1,0:T(2,128)S(1)} %reshape.182), kind=kOutput, calls=%fused_computation.7.clone.clone.1 | convolution fusion | flops 58982544 | bytes 7864416 | tf_op jit(solution)/shard_map/while/body/eval_jaxpr/rjkc,xrjkae->xrace/dot_general | solution.py:30
  376.7 8.6 %select_reduce_fusion.4 = (f32[2]{0:T(128)S(1)}, f32[2]{0:T(128)S(1)}, f32[2,6,128,6,128]{4,3,2,0,1:T(8,128)}) fusion(pred[6,128,6,128]{3,2,1,0:T(8,128)(4,1)S(1)} %copy-done.3, f32[2,6,128,6,128]{4,3,2,0,1:T(8,128)S(1)} %convert_bitcast_fusion.4, f32[2,6,2,2,128,128]{5,3,2,4,0,1:T(2,128)S(1)} %copy.89, s32[6,2,2]{2,1,0:T(2,128)S(1)} %reshape.183), kind=kOutput, calls=%fused_computation.8.clone.clone.1 | convolution fusion | flops 63701132 | bytes 13172848 | tf_op jit(solution)/shard_map/while/body/eval_jaxpr/rjkc,xrjkae->xrace/dot_general | solution.py:30
  385.3 2.1 fusion.127
  387.5 4.2 slice.280
  399.9 5.4 %copy.91 = f32[2,6,128,6,128]{2,1,4,3,0:T(8,128)} copy(f32[2,6,128,6,128]{4,3,2,0,1:T(8,128)} %get-tuple-element.449) | data formatting | bytes 9437184 | tf_op jit(solution)/shard_map/while/body/eval_jaxpr/transpose | solution.py:43
  405.3 7.0 %reshape.184 = f32[2,768,768]{1,2,0:T(8,128)} reshape(f32[2,6,128,6,128]{2,1,4,3,0:T(8,128)} %copy.91) | data formatting | bytes 9437184 | tf_op jit(solution)/shard_map/while/body/eval_jaxpr/transpose | solution.py:43
  412.3 4.4 subtract_reduce_fusion.3
  425.1 2.2 broadcast_compare_fusion.3
  436.9 4.5 copy.89
  447.0 5.8 %copy.87 = f32[2,6,2,2,128,128]{5,3,2,4,0,1:T(2,128)} copy(f32[2,6,2,2,128,128]{4,5,3,2,1,0:T(8,128)} %pad_maximum_fusion.6) | data formatting | bytes 6291456 | tf_op jit(solution)/shard_map/while/body/eval_jaxpr/stack | solution.py:29
  452.8 7.6 %convert_bitcast_fusion.4 = f32[2,6,128,6,128]{4,3,2,0,1:T(8,128)S(1)} fusion(f32[2,6,2,2,128,128]{5,3,2,4,0,1:T(2,128)} %copy.87, s32[6,2,2]{2,1,0:T(2,128)S(1)} %reshape.182), kind=kOutput, calls=%fused_computation.7.clone.clone.1 | convolution fusion | flops 58982544 | bytes 7864416 | tf_op jit(solution)/shard_map/while/body/eval_jaxpr/rjkc,xrjkae->xrace/dot_general | solution.py:30
  460.4 8.6 %select_reduce_fusion.4 = (f32[2]{0:T(128)S(1)}, f32[2]{0:T(128)S(1)}, f32[2,6,128,6,128]{4,3,2,0,1:T(8,128)}) fusion(pred[6,128,6,128]{3,2,1,0:T(8,128)(4,1)S(1)} %copy-done.3, f32[2,6,128,6,128]{4,3,2,0,1:T(8,128)S(1)} %convert_bitcast_fusion.4, f32[2,6,2,2,128,128]{5,3,2,4,0,1:T(2,128)S(1)} %copy.89, s32[6,2,2]{2,1,0:T(2,128)S(1)} %reshape.183), kind=kOutput, calls=%fused_computation.8.clone.clone.1 | convolution fusion | flops 63701132 | bytes 13172848 | tf_op jit(solution)/shard_map/while/body/eval_jaxpr/rjkc,xrjkae->xrace/dot_general | solution.py:30
  469.0 2.1 fusion.127
  471.1 4.2 slice.280
  483.6 5.4 %copy.91 = f32[2,6,128,6,128]{2,1,4,3,0:T(8,128)} copy(f32[2,6,128,6,128]{4,3,2,0,1:T(8,128)} %get-tuple-element.449) | data formatting | bytes 9437184 | tf_op jit(solution)/shard_map/while/body/eval_jaxpr/transpose | solution.py:43
  489.0 7.0 %reshape.184 = f32[2,768,768]{1,2,0:T(8,128)} reshape(f32[2,6,128,6,128]{2,1,4,3,0:T(8,128)} %copy.91) | data formatting | bytes 9437184 | tf_op jit(solution)/shard_map/while/body/eval_jaxpr/transpose | solution.py:43
  496.0 4.4 subtract_reduce_fusion.3
  501.9 2.4 all-reduce
  (232 shorter events, 91.3 us)
Async XLA Ops:
  6.5 1.9 copy-start.6
  6.5 148.7 %all-gather.5.cloned.1.call-start = ((), (), s32[]{:S(2)}) async-start(), calls=%async_computation.1 | async-start | bytes 9437184 | tf_op jit(solution)/shard_map/all_gather | solution.py:60
  7.3 138.4 %copy-start.9 = (s32[1,4,6,2]{2,3,1,0:T(2,128)S(1)}, s32[1,4,6,2]{2,3,1,0:T(2,128)}, u32[]{:S(2)}) copy-start(s32[1,4,6,2]{2,3,1,0:T(2,128)} %param.12) | copy-start | bytes 580
  7.3 144.6 %copy-start.11 = (u32[32]{0:T(128)S(1)}, u32[32]{0:T(128)}, u32[]{:S(2)}) copy-start(u32[32]{0:T(128)} %constant.152) | copy-start | bytes 388
  7.3 145.3 %copy-start.10 = (s32[4]{0:T(128)S(1)}, s32[4]{0:T(128)}, u32[]{:S(2)}) copy-start(s32[4]{0:T(128)} %param.14) | copy-start | bytes 52
  7.3 157.6 %all-gather.3.cloned.1.call-start = ((), (), s32[]{:S(2)}) async-start(), calls=%async_computation | async-start | bytes 9437184 | tf_op jit(solution)/shard_map/all_gather | solution.py:62
  8.4 137.2 %collective-permute-start = (bf16[1,4,2,6,2,128,128]{6,5,4,3,2,0,1:T(8,128)(2,1)S(1)}, bf16[1,4,2,6,2,128,128]{6,5,4,3,2,0,1:T(8,128)(2,1)}, u32[]{:S(2)}, u32[]{:S(2)}) collective-permute-start(bf16[1,4,2,6,2,128,128]{6,5,4,3,2,0,1:T(8,128)(2,1)S(1)} %bitcast.291), channel_id=1, source_target_pairs={{0,8},{2,10},{4,12},{6,14},{8,0},{10,2},{12,4},{14,6},{1,9},{3,11}... | collective-permute-start | bytes 9437192 | tf_op jit(solution)/shard_map/ppermute | solution.py:10
  145.7 7.5 %collective-permute-start.1 = (s32[1,4,6,2]{2,3,0,1:T(2,128)S(1)}, s32[1,4,6,2]{2,3,0,1:T(2,128)S(1)}, u32[]{:S(2)}, u32[]{:S(2)}) collective-permute-start(s32[1,4,6,2]{2,3,0,1:T(2,128)S(1)} %bitcast.294), channel_id=1, source_target_pairs={{0,8},{2,10},{4,12},{6,14},{8,0},{10,2},{12,4},{14,6},{1,9},{3,11}... | collective-permute-start | bytes 584 | tf_op jit(solution)/shard_map/ppermute | solution.py:10
  151.8 3.2 copy-start.7
  155.1 11.9 %copy-start.8 = (s32[1,1,6,2]{3,2,1,0:T(8,128)}, s32[1,1,6,2]{3,2,1,0:T(8,128)S(1)}, u32[]{:S(2)}) copy-start(s32[1,1,6,2]{3,2,1,0:T(8,128)S(1)} %copy.58) | copy-start | bytes 148
  181.1 1.1 copy-start.5
  190.3 1.8 copy-start.2
  190.3 1.8 copy-start.4
  192.6 1.1 copy-start.1
  201.7 7.6 %copy-start.3 = (pred[6,128,6,128]{3,2,1,0:T(8,128)(4,1)S(1)}, pred[6,128,6,128]{3,2,1,0:T(8,128)(4,1)}, u32[]{:S(2)}) copy-start(pred[6,128,6,128]{3,2,1,0:T(8,128)(4,1)} %broadcast_compare_fusion.3) | copy-start | bytes 1769476 | tf_op jit(solution)/shard_map/while
  237.9 7.0 %copy-start = (f32[1,768,768]{2,1,0:T(8,128)S(1)}, f32[1,768,768]{2,1,0:T(8,128)}, u32[]{:S(2)}) copy-start(f32[1,768,768]{2,1,0:T(8,128)} %slice.280) | copy-start | bytes 7077892 | tf_op jit(solution)/shard_map/while
  264.8 1.1 copy-start.5
  274.0 1.8 copy-start.2
  274.0 1.8 copy-start.4
  276.2 1.1 copy-start.1
  285.4 7.6 %copy-start.3 = (pred[6,128,6,128]{3,2,1,0:T(8,128)(4,1)S(1)}, pred[6,128,6,128]{3,2,1,0:T(8,128)(4,1)}, u32[]{:S(2)}) copy-start(pred[6,128,6,128]{3,2,1,0:T(8,128)(4,1)} %broadcast_compare_fusion.3) | copy-start | bytes 1769476 | tf_op jit(solution)/shard_map/while
  321.6 7.0 %copy-start = (f32[1,768,768]{2,1,0:T(8,128)S(1)}, f32[1,768,768]{2,1,0:T(8,128)}, u32[]{:S(2)}) copy-start(f32[1,768,768]{2,1,0:T(8,128)} %slice.280) | copy-start | bytes 7077892 | tf_op jit(solution)/shard_map/while
  348.5 1.1 copy-start.5
  357.7 1.8 copy-start.2
  357.7 1.8 copy-start.4
  359.9 1.1 copy-start.1
  369.1 7.6 %copy-start.3 = (pred[6,128,6,128]{3,2,1,0:T(8,128)(4,1)S(1)}, pred[6,128,6,128]{3,2,1,0:T(8,128)(4,1)}, u32[]{:S(2)}) copy-start(pred[6,128,6,128]{3,2,1,0:T(8,128)(4,1)} %broadcast_compare_fusion.3) | copy-start | bytes 1769476 | tf_op jit(solution)/shard_map/while
  405.3 7.0 %copy-start = (f32[1,768,768]{2,1,0:T(8,128)S(1)}, f32[1,768,768]{2,1,0:T(8,128)}, u32[]{:S(2)}) copy-start(f32[1,768,768]{2,1,0:T(8,128)} %slice.280) | copy-start | bytes 7077892 | tf_op jit(solution)/shard_map/while
  432.2 1.1 copy-start.5
  441.4 1.8 copy-start.2
  441.4 1.8 copy-start.4
  443.6 1.1 copy-start.1
  452.8 7.6 %copy-start.3 = (pred[6,128,6,128]{3,2,1,0:T(8,128)(4,1)S(1)}, pred[6,128,6,128]{3,2,1,0:T(8,128)(4,1)}, u32[]{:S(2)}) copy-start(pred[6,128,6,128]{3,2,1,0:T(8,128)(4,1)} %broadcast_compare_fusion.3) | copy-start | bytes 1769476 | tf_op jit(solution)/shard_map/while
  489.0 7.0 %copy-start = (f32[1,768,768]{2,1,0:T(8,128)S(1)}, f32[1,768,768]{2,1,0:T(8,128)}, u32[]{:S(2)}) copy-start(f32[1,768,768]{2,1,0:T(8,128)} %slice.280) | copy-start | bytes 7077892 | tf_op jit(solution)/shard_map/while
Sparse Core Ops, SparseCore 0:
  8.9 18.1 all-gather.4
  145.8 19.0 all-gather.2
where the time goes:
time: 516 us; the launch traced here: 512 us
  local copies, waits for them, and re-layouts  171 us (33%)
  waiting for transfers between devices  143 us (28%)
  matrix products  83.4 us (16%)
  other arithmetic  43.9 us (9%)
  loops' own time  43.5 us (8%)
  between operations  14.8 us (3%)
  starting transfers between devices  6.18 us (1%)
  blocking collectives  6.04 us (1%)
    ppermute x2, waiting for transfers between devices, from_partner(): return lax.ppermute(value, axis, pairs)  135 us
    dot_general x8, matrix products, block_product(): jnp.einsum('rjkc,xrjkae->xrace', onehot, stacked, precision=lax.Precision...  64.9 us
    transpose x8, local copies, waits for them, and re-layouts, pair_term(): second_flip = jnp.swapaxes(second_wide, 1, 2)  49.8 us
    another operation x1, loops' own time, local(): lax.map(one_item, jnp.arange(slot_count * delta_count, dtype=jnp.int32))  43.5 us
    another operation x8, local copies, waits for them, and re-layouts, block_product(): stacked = jnp.stack([real_part, imag_part])  41.1 us
    reduce_sum x4, other arithmetic, pair_term(): jnp.sum(first_wide[0] * second_flip[0] - first_wide[1] * second_flip[1])  17.5 us
    slice x4, local copies, waits for them, and re-layouts, pair_term(): first_wide[1] * second_flip[1]  16.6 us
    slice x8, local copies, waits for them, and re-layouts, pair_term(): first_wide[0] * second_flip[0] - first_wide[1] * second_flip[1]  15.6 us
  transfers between devices with their start and end apart: 4, of which 2 were waited for; matrix products, arithmetic and copies ran while one was open for 1% of the time, Pallas kernels for 0%

commit v1 on v0

v1 whole, which is shorter than its diff:
```python
import functools

import jax
import jax.numpy as jnp
from jax import lax
from jax.experimental import pallas as pl
from jax.experimental.pallas import tpu as pltpu
from jax.sharding import PartitionSpec as P

F32 = jnp.float32
BF16 = jnp.bfloat16


def one_way_pairs(count):
    half = count // 2
    outer = half // 2
    return [(g + half, g) if g < outer else (g, g + half) for g in range(half)]


def weights_kernel(
    order_ref, a_cols, d_cols, b_cols, m_cols, a_ref, d_ref, b_ref, u_ref, la, ld, bs, yacc, yn, uacc
):
    slot = pl.program_id(0)
    rows, per_row, size = a_ref.shape[1], a_ref.shape[2], a_ref.shape[3]
    base = slot * rows * per_row
    lo, hi = pl.ds(0, size), pl.ds(size, size)

    @pl.when(slot == 0)
    def _():
        for r in range(rows):
            for j in range(per_row):
                real, imag = a_ref[0, r, j], a_ref[1, r, j]
                la[r, j, lo, lo] = real
                la[r, j, lo, hi] = -imag
                la[r, j, hi, lo] = imag
                la[r, j, hi, hi] = real
                real, imag = d_ref[0, r, j].T, d_ref[1, r, j].T
                up, down = pl.ds(2 * j * size, size), pl.ds((2 * j + 1) * size, size)
                ld[r, up, lo] = real
                ld[r, up, hi] = -imag
                ld[r, down, lo] = imag
                ld[r, down, hi] = real

    for r in range(rows):
        for j in range(per_row):
            bs[r, lo, pl.ds(j * size, size)] = b_ref[0, 0, r, j]
            bs[r, hi, pl.ds(j * size, size)] = b_ref[0, 1, r, j]

    yacc[...] = jnp.zeros_like(yacc)
    for r in range(rows):
        for j in range(per_row):
            inner = a_cols[r * per_row + j]
            part = jnp.dot(la[r, j], bs[inner], preferred_element_type=F32)
            for k in range(per_row):
                col = b_cols[base + inner * per_row + k]
                yacc[r, col] += part[:, k * size : (k + 1) * size]

    diagonal = lax.broadcasted_iota(jnp.int32, (size, size), 0) == lax.broadcasted_iota(
        jnp.int32, (size, size), 1
    )
    trace_real = jnp.zeros((size, size), F32)
    trace_imag = jnp.zeros((size, size), F32)
    for col in range(rows):
        for r in range(rows):
            real = yacc[r, col, lo].astype(BF16)
            imag = yacc[r, col, hi].astype(BF16)
            yn[col, pl.ds(r * size, size), lo] = real
            yn[col, pl.ds(r * size, size), hi] = imag
            if r == col:
                trace_real += real.astype(F32)
                trace_imag += imag.astype(F32)
    trace_real = jnp.sum(jnp.where(diagonal, trace_real, 0.0))
    trace_imag = jnp.sum(jnp.where(diagonal, trace_imag, 0.0))

    uacc[...] = jnp.zeros_like(uacc)
    wide = 2 if rows % 2 == 0 else 1
    for r in range(rows):
        for pair in range(rows // wide):
            part = lax.dot_general(
                ld[r],
                yn[r, pl.ds(pair * wide * size, wide * size)],
                (((1,), (1,)), ((), ())),
                preferred_element_type=F32,
            )
            for j in range(per_row):
                row = d_cols[r * per_row + j]
                for k in range(wide):
                    uacc[row, pair * wide + k] += part[
                        2 * j * size : 2 * (j + 1) * size, k * size : (k + 1) * size
                    ]

    for r in range(rows):
        for j in range(per_row):
            col = m_cols[base + r * per_row + j]
            pick = jnp.int32(0)
            found = jnp.int32(0)
            for k in range(per_row):
                hit = d_cols[col * per_row + k] == r
                pick = jnp.where(hit, k, pick)
                found = jnp.where(hit, 1, found)
            keep = found.astype(F32)
            at = pl.multiple_of(pick * 2 * size, 2 * size)
            real = ld[col, pl.ds(at, size), lo].astype(F32)
            imag = ld[col, pl.ds(at + size, size), lo].astype(F32)
            weight_real, weight_imag = trace_real * keep, trace_imag * keep
            u_ref[0, r, j, 0] = weight_real * real - weight_imag * imag - uacc[r, col, lo]
            u_ref[0, r, j, 1] = weight_real * imag + weight_imag * real - uacc[r, col, hi]


def weights(order, a_cols, d_cols, b_cols, m_cols, a, d, fields):
    times = fields.shape[0]
    _, rows, per_row, size, _ = a.shape
    whole = lambda slot, *_: (0, 0, 0, 0, 0)
    return pl.pallas_call(
        weights_kernel,
        out_shape=jax.ShapeDtypeStruct((times, rows, per_row, 2, size, size), F32),
        grid_spec=pltpu.PrefetchScalarGridSpec(
            num_scalar_prefetch=5,
            grid=(times,),
            in_specs=[
                pl.BlockSpec(a.shape, whole),
                pl.BlockSpec(a.shape, whole),
                pl.BlockSpec((1,) + a.shape, lambda slot, order, *_: (order[slot], 0, 0, 0, 0, 0)),
            ],
            out_specs=pl.BlockSpec(
                (1, rows, per_row, 2, size, size), lambda slot, *_: (slot, 0, 0, 0, 0, 0)
            ),
            scratch_shapes=[
                pltpu.VMEM((rows, per_row, 2 * size, 2 * size), BF16),
                pltpu.VMEM((rows, per_row * 2 * size, 2 * size), BF16),
                pltpu.VMEM((rows, 2 * size, per_row * size), BF16),
                pltpu.VMEM((rows, rows, 2 * size, size), F32),
                pltpu.VMEM((rows, rows * size, 2 * size), BF16),
                pltpu.VMEM((rows, rows, 2 * size, size), F32),
            ],
        ),
        compiler_params=pltpu.CompilerParams(vmem_limit_bytes=40 * 2**20),
        cost_estimate=pl.CostEstimate(
            flops=times * 1_600_000_000, bytes_accessed=times * 8_000_000, transcendentals=0
        ),
        name="weights",
    )(order, a_cols, d_cols, b_cols, m_cols, a, d, fields)


def products(field_ref, u_refs, acc):
    per_row, size = field_ref.shape[2], field_ref.shape[3]
    for j in range(per_row):
        real = field_ref[0, 0, j].astype(F32)
        imag = field_ref[1, 0, j].astype(F32)
        for s, u_ref in enumerate(u_refs):
            u_real, u_imag = u_ref[0, 0, j, 0], u_ref[0, 0, j, 1]
            fold = lambda x: jnp.sum(x.reshape(size // 8, 8, size), axis=0)
            acc[2 * s] += fold(real * u_real - imag * u_imag)
            acc[2 * s + 1] += fold(real * u_imag + imag * u_real)


def inner_kernel(field_ref, u0_ref, u1_ref, out_ref):
    @pl.when(pl.program_id(0) == 0)
    def _():
        out_ref[...] = jnp.zeros_like(out_ref)

    products(field_ref, (u0_ref, u1_ref), out_ref)


def last_kernel(times_ref, sinks_ref, *refs):
    *earlier, field_ref, u0_ref, u1_ref, out_ref, acc = refs
    slots = len(earlier) + 1
    deltas = out_ref.shape[0] // 2

    @pl.when(pl.program_id(0) == 0)
    def _():
        acc[...] = jnp.zeros_like(acc)

    products(field_ref, (u0_ref, u1_ref), acc)

    @pl.when(pl.program_id(0) == pl.num_programs(0) - 1)
    def _():
        lines = [jnp.zeros((8, acc.shape[2]), F32) for _ in range(2 * deltas)]
        for slot in range(slots):
            held = acc if slot == slots - 1 else earlier[slot]
            for s in range(2):
                for k in range(deltas):
                    keep = (sinks_ref[s * deltas + k] == times_ref[slot]).astype(F32)
                    for part in range(2):
                        lines[part * deltas + k] += keep * held[2 * s + part]
        table = jnp.concatenate([jnp.sum(line, axis=0, keepdims=True) for line in lines], axis=0)
        out_ref[...] = jnp.broadcast_to(jnp.sum(table, axis=1, keepdims=True), out_ref.shape)


def field_specs(field, slot):
    _, rows, per_row, size, _ = field.shape
    return [
        pl.BlockSpec((2, 1, per_row, size, size), lambda r, *_: (0, r, 0, 0, 0)),
        pl.BlockSpec((1, 1, per_row, 2, size, size), lambda r, *_: (slot, r, 0, 0, 0, 0)),
        pl.BlockSpec((1, 1, per_row, 2, size, size), lambda r, *_: (slot, r, 0, 0, 0, 0)),
    ]


def inner(field, u0, u1, slot):
    rows, size = field.shape[1], field.shape[3]
    return pl.pallas_call(
        inner_kernel,
        out_shape=jax.ShapeDtypeStruct((4, 8, size), F32),
        grid=(rows,),
        in_specs=field_specs(field, slot),
        out_specs=pl.BlockSpec((4, 8, size), lambda r: (0, 0, 0)),
        cost_estimate=pl.CostEstimate(flops=4_000_000, bytes_accessed=4_000_000, transcendentals=0),
        name="inner",
    )(field, u0, u1)


def last(times, sinks, earlier, field, u0, u1):
    rows, size = field.shape[1], field.shape[3]
    lines = sinks.shape[0]
    whole = pl.BlockSpec((4, 8, size), lambda r, *_: (0, 0, 0))
    return pl.pallas_call(
        last_kernel,
        out_shape=jax.ShapeDtypeStruct((lines, size), F32),
        grid_spec=pltpu.PrefetchScalarGridSpec(
            num_scalar_prefetch=2,
            grid=(rows,),
            in_specs=[whole] * len(earlier) + field_specs(field, len(earlier)),
            out_specs=pl.BlockSpec((lines, size), lambda r, *_: (0, 0)),
            scratch_shapes=[pltpu.VMEM((4, 8, size), F32)],
        ),
        cost_estimate=pl.CostEstimate(flops=4_000_000, bytes_accessed=4_000_000, transcendentals=0),
        name="last",
    )(times, sinks, *earlier, field, u0, u1)


def local(fields, block_cols, sources, deltas, partner):
    assert fields.shape[0] == 1 and lax.axis_size("src") == 2
    del partner
    fields, block_cols = fields[0], block_cols[0]
    times, _, rows, per_row, size, _ = fields.shape
    per_field = rows * per_row
    total_times = 2 * times
    delta_count = deltas.shape[0]
    core = lax.axis_index("src")
    pairs = one_way_pairs(lax.axis_size("mom"))
    swap = lambda value: lax.ppermute(value, "src", [(0, 1), (1, 0)])
    to_partner = lambda value: lax.ppermute(value, "mom", pairs)

    source = sources[0] - core * times
    order = (source + jnp.arange(times, dtype=jnp.int32)) % times
    picked = [lax.dynamic_index_in_dim(fields, order[i], 0, keepdims=False) for i in range(times)]
    far = [to_partner(field) for field in picked]

    cols = jnp.take(block_cols.reshape(times, per_field), order, axis=0).reshape(-1)
    pack = jnp.concatenate([cols, sources])
    other_pack = swap(pack)
    far_pack, far_other_pack = jnp.split(to_partner(jnp.concatenate([pack, other_pack])), 2)
    m_cols = far_pack[:-1]
    other_source = other_pack[-1]
    other_field = swap(picked[0])
    far_other = swap(far[0])

    u0 = weights(order, far_pack[:per_field], cols[:per_field], cols, m_cols, far[0], picked[0], fields)
    u1 = weights(
        order, far_other_pack[:per_field], other_pack[:per_field], cols, m_cols, far_other, other_field, fields
    )
    sinks = jnp.concatenate(
        [(sources[0] + deltas) % total_times, (other_source + deltas) % total_times]
    )
    slot_times = order + core * times
    earlier = [inner(far[i], u0, u1, i) for i in range(times - 1)]
    own = last(slot_times, sinks, earlier, far[-1], u0, u1)

    both = ("mom", "src")
    straight = [(2 * a + c, 2 * b + c) for b, a in pairs for c in range(2)]
    crossed = [(2 * a + c, 2 * b + 1 - c) for b, a in pairs for c in range(2)]
    total = own + swap(own) + lax.ppermute(own, both, straight) + lax.ppermute(own, both, crossed)
    total = total[:, :1].reshape(2, delta_count, 1)
    share = delta_count // 2
    return lax.dynamic_slice_in_dim(total, core * share, share, axis=1)


def solution(mesh):
    in_specs = (
        P(("ens", "mom"), "src", None, None, None, None, None),
        P(("ens", "mom"), "src", None, None),
        P("src"),
        P(),
        P("mom"),
    )
    out_specs = P(None, "src", ("ens", "mom"))
    return jax.shard_map(local, mesh=mesh, in_specs=in_specs, out_specs=out_specs, check_vma=False)
```

time: 516 us -> 147 us (0.28)
  local copies, waits for them, and re-layouts: 171 us -> 12 us
  waiting for transfers between devices: 143 us -> 46 us
  matrix products: 83.4 us -> 0 us
  Pallas kernels: 0 us -> 56 us
  loops' own time: 43.5 us -> 0 us
  other arithmetic: 43.9 us -> 2.73 us
  starting transfers between devices: 6.18 us -> 20.6 us
  between operations: 14.8 us -> 8.36 us
  blocking collectives: 6.04 us -> 0 us
    ppermute x2 -> x11, waiting for transfers between devices: 135 us -> 46 us  [the longest x5 41.1 us: local(): to_partner = lambda value: lax.ppermute(value, 'mom', pairs)]
    dot_general x40 -> x0, matrix products: 83.4 us -> none  [the longest x8 64.9 us: block_product(): jnp.einsum('rjkc,xrjkae->xrace', onehot, stacked, precision=lax.Precision...]
    pallas_call x0 -> x6, Pallas kernels: none -> 56 us  [the longest x2 37.5 us: weights(): pl.pallas_call(weights_kernel, out_shape=jax.ShapeDtypeStruct((times, row...]
    transpose x8 -> x0, local copies, waits for them, and re-layouts: 49.8 us -> none  [pair_term(): second_flip = jnp.swapaxes(second_wide, 1, 2)]
    another operation x1 -> x0, loops' own time: 43.5 us -> none  [local(): lax.map(one_item, jnp.arange(slot_count * delta_count, dtype=jnp.int32))]
    slice x28 -> x5, local copies, waits for them, and re-layouts: 42.6 us -> 1.51 us  [the longest x1 0.67 us: local(): order[i]]
    another operation x8 -> x2, local copies, waits for them, and re-layouts: 41.1 us -> 0.11 us  [local(): block_cols.reshape(times, per_field)]
    reduce_sum x4 -> x0, other arithmetic: 17.5 us -> none  [pair_term(): jnp.sum(first_wide[0] * second_flip[0] - first_wide[1] * second_flip[1])]
  transfers between devices with their start and end apart: 4 -> 11, of which waited for: 2 -> 3; matrix products, arithmetic and copies ran while one was open for 1% -> 2% of each run, Pallas kernels for 0% -> 35%
where the time goes in v1:
time: 147 us; the launch traced here: 146 us
  Pallas kernels  56 us (38%)
  waiting for transfers between devices  46 us (31%)
  starting transfers between devices  20.6 us (14%)
  local copies, waits for them, and re-layouts  12 us (8%)
  between operations  8.36 us (6%)
  other arithmetic  2.73 us (2%)
    ppermute x5, waiting for transfers between devices, local(): to_partner = lambda value: lax.ppermute(value, 'mom', pairs)  41.1 us
    pallas_call x2, Pallas kernels, weights(): pl.pallas_call(weights_kernel, out_shape=jax.ShapeDtypeStruct((times, row...  37.5 us
    ppermute x5, starting transfers between devices, local(): to_partner = lambda value: lax.ppermute(value, 'mom', pairs)  17.2 us
    pallas_call x3, Pallas kernels, inner(): pl.pallas_call(inner_kernel, out_shape=jax.ShapeDtypeStruct((4, 8, size),...  13.2 us
    unnamed x11, local copies, waits for them, and re-layouts  5.39 us
    pallas_call x1, Pallas kernels, last(): pl.pallas_call(last_kernel, out_shape=jax.ShapeDtypeStruct((lines, size),...  5.28 us
    squeeze x1, local copies, waits for them, and re-layouts, local(): lax.dynamic_index_in_dim(fields, order[i], 0, keepdims=False)  3.66 us
  transfers between devices with their start and end apart: 11, of which 3 were waited for; matrix products, arithmetic and copies ran while one was open for 2% of the time, Pallas kernels for 35%

profile of v1, /device:TPU:8, one launch (start us, length us, event | category | flops | bytes accessed | tf_op | source)
XLA Modules:
  0.0 145.7 jit_solution(14459958524327213433)
XLA Ops:
  0.8 0.7 fusion.5
  8.9 3.7 %dynamic-slice_bitcast_fusion = (bf16[2,6,2,128,128]{4,3,2,1,0:T(8,128)(2,1)}, bf16[2,6,2,128,128]{4,3,2,1,0:T(8,128)(2,1)}, bf16[2,6,2,128,128]{4,3,2,1,0:T(8,128)(2,1)}, bf16[2,6,2,128,128]{4,3,2,1,0:T(8,128)(2,1)}) fusion(bf16[1,4,2,6,2,128,128]{6,5,4,3,2,1,0:T(8,128)(2,1)} %param.5, s32[]{:T(128)S(6)} %select_n.68, s32[]{:T(128)S(6)} %select_n.66, ...), kind=kLoop, calls=%fused_computation.1 | loop fusion | bytes 6291472 | tf_op jit(solution)/shard_map/jit(dynamic_index_in_dim)/squeeze | solution.py:246
  12.6 0.0 collective-permute-start.4
  12.6 5.4 %collective-permute-start.1 = (bf16[2,6,2,128,128]{4,3,2,1,0:T(8,128)(2,1)}, bf16[2,6,2,128,128]{4,3,2,1,0:T(8,128)(2,1)}, u32[]{:S(2)}, u32[]{:S(2)}) collective-permute-start(bf16[2,6,2,128,128]{4,3,2,1,0:T(8,128)(2,1)} %get-tuple-element.7.d_ref), channel_id=1, source_target_pairs={{8,0},{10,2},{4,12},{6,14},{9,1},{11,3},{5,13},{7,15},{24,16},{26,... | collective-permute-start | bytes 2359304 | tf_op jit(solution)/shard_map/ppermute | solution.py:242
  18.0 0.1 copy.8
  18.2 0.1 copy.9
  18.3 0.6 gather_fusion
  18.8 0.1 broadcast_select_fusion
  18.9 0.1 select_n.63.b_cols
  19.0 0.1 pad_add_fusion
  19.0 0.2 collective-permute-start
  19.3 2.2 %collective-permute-start.7 = (bf16[2,6,2,128,128]{4,3,2,1,0:T(8,128)(2,1)}, bf16[2,6,2,128,128]{4,3,2,1,0:T(8,128)(2,1)}, u32[]{:S(2)}, u32[]{:S(2)}) collective-permute-start(bf16[2,6,2,128,128]{4,3,2,1,0:T(8,128)(2,1)} %get-tuple-element.5), channel_id=1, source_target_pairs={{8,0},{10,2},{4,12},{6,14},{9,1},{11,3},{5,13},{7,15},{24,16},{26,... | collective-permute-start | bytes 2359304 | tf_op jit(solution)/shard_map/ppermute | solution.py:242
  21.5 2.2 %collective-permute-start.5 = (bf16[2,6,2,128,128]{4,3,2,1,0:T(8,128)(2,1)}, bf16[2,6,2,128,128]{4,3,2,1,0:T(8,128)(2,1)}, u32[]{:S(2)}, u32[]{:S(2)}) collective-permute-start(bf16[2,6,2,128,128]{4,3,2,1,0:T(8,128)(2,1)} %get-tuple-element.6), channel_id=1, source_target_pairs={{8,0},{10,2},{4,12},{6,14},{9,1},{11,3},{5,13},{7,15},{24,16},{26,... | collective-permute-start | bytes 2359304 | tf_op jit(solution)/shard_map/ppermute | solution.py:242
  23.7 0.5 broadcast_add_fusion.times_ref
  24.2 0.0 collective-permute-done
  24.2 0.1 pad_add_fusion.2
  24.3 1.3 collective-permute-start.2
  25.6 0.6 slice.39
  26.2 0.6 and_select_fusion.2
  26.9 0.6 pad_add_fusion.1.sinks_ref
  27.4 41.1 %collective-permute-done.2 = s32[98]{0:T(128)S(1)} collective-permute-done((s32[98]{0:T(128)S(1)}, s32[98]{0:T(128)S(1)}, u32[]{:S(2)}, u32[]{:S(2)}) %collective-permute-start.2) | collective-permute-done | bytes 424 | tf_op jit(solution)/shard_map/ppermute | solution.py:242
  68.6 6.2 %collective-permute-start.6 = (bf16[2,6,2,128,128]{4,3,2,1,0:T(8,128)(2,1)}, bf16[2,6,2,128,128]{4,3,2,1,0:T(8,128)(2,1)}, u32[]{:S(2)}, u32[]{:S(2)}) collective-permute-start(bf16[2,6,2,128,128]{4,3,2,1,0:T(8,128)(2,1)} %get-tuple-element.8), channel_id=1, source_target_pairs={{8,0},{10,2},{4,12},{6,14},{9,1},{11,3},{5,13},{7,15},{24,16},{26,... | collective-permute-start | bytes 2359304 | tf_op jit(solution)/shard_map/ppermute | solution.py:242
  74.8 0.0 collective-permute-done.1.a_ref.field_ref
  74.8 0.0 collective-permute-start.3
  74.8 0.1 fusion.6
  74.8 18.9 %weights.2.u0_ref.refs_4_ = f32[4,6,2,2,128,128]{5,4,3,2,1,0:T(8,128)S(1)} custom-call(s32[4]{0:T(128)S(1)} %and_select_fusion.3.order_ref, s32[12]{0:T(128)S(1)} %get-tuple-element.14.a_cols, s32[12]{0:T(128)S(1)} %slice_bitcast_fusion.d_cols, s32[48]{0:T(128)S(1)} %select_n.63.b_cols, s32[48]{0:T(128)S(1)} %bitcast.28, ...), custom_call_target="tpu_custom_call" | custom-call | flops 6400000000 | bytes 32000000 | tf_op jit(solution)/shard_map/weights/pallas_call | solution.py:114
  93.7 2.7 %copy-done = f32[4,6,2,2,128,128]{5,4,3,2,1,0:T(8,128)} copy-done((f32[4,6,2,2,128,128]{5,4,3,2,1,0:T(8,128)}, f32[4,6,2,2,128,128]{5,4,3,2,1,0:T(8,128)S(1)}, u32[]{:S(2)}) %copy-start) | copy-done | bytes 6291480
  96.4 0.0 collective-permute-done.4.d_ref
  96.4 0.0 collective-permute-done.3.a_ref
  96.4 18.7 %weights.3.u1_ref.refs_5_ = f32[4,6,2,2,128,128]{5,4,3,2,1,0:T(8,128)S(1)} custom-call(s32[4]{0:T(128)S(1)} %and_select_fusion.3.order_ref, s32[12]{0:T(128)S(1)} %get-tuple-element.13.a_cols, s32[12]{0:T(128)S(1)} %bitcast.30, s32[48]{0:T(128)S(1)} %select_n.63.b_cols, s32[48]{0:T(128)S(1)} %bitcast.29, ...), custom_call_target="tpu_custom_call" | custom-call | flops 6400000000 | bytes 32000000 | tf_op jit(solution)/shard_map/weights/pallas_call | solution.py:114
  115.1 2.6 %copy-done.1 = f32[4,6,2,2,128,128]{5,4,3,2,1,0:T(8,128)} copy-done((f32[4,6,2,2,128,128]{5,4,3,2,1,0:T(8,128)}, f32[4,6,2,2,128,128]{5,4,3,2,1,0:T(8,128)S(1)}, u32[]{:S(2)}) %copy-start.1) | copy-done | bytes 6291480
  117.7 4.4 %inner.3.refs_0_ = f32[4,8,128]{2,1,0:T(8,128)} custom-call(bf16[2,6,2,128,128]{4,3,2,1,0:T(8,128)(2,1)} %collective-permute-done.1.a_ref.field_ref, f32[4,6,2,2,128,128]{5,4,3,2,1,0:T(8,128)} %copy-done, f32[4,6,2,2,128,128]{5,4,3,2,1,0:T(8,128)} %copy-done.1), custom_call_target="tpu_custom_call" | custom-call | flops 4000000 | bytes 4000000 | tf_op jit(solution)/shard_map/inner/pallas_call | solution.py:201
  122.1 0.0 collective-permute-done.6.field_ref
  122.1 4.4 %inner.5.refs_2_ = f32[4,8,128]{2,1,0:T(8,128)} custom-call(bf16[2,6,2,128,128]{4,3,2,1,0:T(8,128)(2,1)} %collective-permute-done.6.field_ref, f32[4,6,2,2,128,128]{5,4,3,2,1,0:T(8,128)} %copy-done, f32[4,6,2,2,128,128]{5,4,3,2,1,0:T(8,128)} %copy-done.1), custom_call_target="tpu_custom_call" | custom-call | flops 4000000 | bytes 4000000 | tf_op jit(solution)/shard_map/inner/pallas_call | solution.py:201
  126.5 0.0 collective-permute-done.5.field_ref
  126.5 4.4 %inner.4.refs_1_ = f32[4,8,128]{2,1,0:T(8,128)} custom-call(bf16[2,6,2,128,128]{4,3,2,1,0:T(8,128)(2,1)} %collective-permute-done.5.field_ref, f32[4,6,2,2,128,128]{5,4,3,2,1,0:T(8,128)} %copy-done, f32[4,6,2,2,128,128]{5,4,3,2,1,0:T(8,128)} %copy-done.1), custom_call_target="tpu_custom_call" | custom-call | flops 4000000 | bytes 4000000 | tf_op jit(solution)/shard_map/inner/pallas_call | solution.py:201
  130.9 0.0 collective-permute-done.7.refs_3_
  130.9 5.3 %last.1 = f32[8,128]{1,0:T(8,128)} custom-call(s32[4]{0:T(128)} %broadcast_add_fusion.times_ref, s32[8]{0:T(128)} %pad_add_fusion.1.sinks_ref, f32[4,8,128]{2,1,0:T(8,128)} %inner.3.refs_0_, f32[4,8,128]{2,1,0:T(8,128)} %inner.4.refs_1_, f32[4,8,128]{2,1,0:T(8,128)} %inner.5.refs_2_, bf16[2,6,2,128,128]{4,3,2,1,0:T(8,128)(2,1)} %collective-permute-done.7.refs_3_, ...), custom_call_target="tpu_custom_call" | custom-call | flops 4000000 | bytes 4000000 | tf_op jit(solution)/shard_map/last/pallas_call | solution.py:216
  136.2 1.3 collective-permute-start.10
  137.5 1.3 collective-permute-start.9
  138.8 0.6 collective-permute-start.8
  139.4 2.9 %collective-permute-done.10 = f32[8,128]{1,0:T(8,128)S(1)} collective-permute-done((f32[8,128]{1,0:T(8,128)}, f32[8,128]{1,0:T(8,128)S(1)}, u32[]{:S(2)}, u32[]{:S(2)}) %collective-permute-start.10) | collective-permute-done | bytes 4128 | tf_op jit(solution)/shard_map/ppermute | solution.py:272
  142.2 2.0 %collective-permute-done.9 = f32[8,128]{1,0:T(8,128)S(1)} collective-permute-done((f32[8,128]{1,0:T(8,128)}, f32[8,128]{1,0:T(8,128)S(1)}, u32[]{:S(2)}, u32[]{:S(2)}) %collective-permute-start.9) | collective-permute-done | bytes 4128 | tf_op jit(solution)/shard_map/ppermute | solution.py:272
  144.2 0.0 collective-permute-done.8
  144.2 0.7 add_add_fusion
  144.9 0.1 slice_reduce_fusion
  145.0 0.1 reshape.71
  145.1 0.6 constant_dynamic-slice_fusion
  (14 shorter events, 0.1 us)
Async XLA Ops:
  0.0 74.8 %copy-start.2 = (bf16[1,4,2,6,2,128,128]{6,5,4,3,2,1,0:T(8,128)(2,1)S(1)}, bf16[1,4,2,6,2,128,128]{6,5,4,3,2,1,0:T(8,128)(2,1)}, u32[]{:S(2)}) copy-start(bf16[1,4,2,6,2,128,128]{6,5,4,3,2,1,0:T(8,128)(2,1)} %param.5) | copy-start | bytes 9437188
  0.0 18.0 %copy-start.3 = (s32[1,4,6,2]{2,3,1,0:T(2,128)S(1)}, s32[1,4,6,2]{2,3,1,0:T(2,128)}, u32[]{:S(2)}) copy-start(s32[1,4,6,2]{2,3,1,0:T(2,128)} %param.6) | copy-start | bytes 580
  0.0 26.2 %copy-start.4 = (s32[4]{0:T(128)S(1)}, s32[4]{0:T(128)}, u32[]{:S(2)}) copy-start(s32[4]{0:T(128)} %param.8) | copy-start | bytes 52
  12.6 83.8 %collective-permute-start.4 = (bf16[2,6,2,128,128]{4,3,2,1,0:T(8,128)(2,1)}, bf16[2,6,2,128,128]{4,3,2,1,0:T(8,128)(2,1)}, u32[]{:S(2)}, u32[]{:S(2)}) collective-permute-start(bf16[2,6,2,128,128]{4,3,2,1,0:T(8,128)(2,1)} %get-tuple-element.7.d_ref), channel_id=1, source_target_pairs={{0,1},{1,0},{2,3},{3,2},{4,5},{5,4},{6,7},{7,6},{8,9},{9,8},{10,11... | collective-permute-start | bytes 2359304 | tf_op jit(solution)/shard_map/ppermute | solution.py:241
  12.6 62.1 %collective-permute-start.1 = (bf16[2,6,2,128,128]{4,3,2,1,0:T(8,128)(2,1)}, bf16[2,6,2,128,128]{4,3,2,1,0:T(8,128)(2,1)}, u32[]{:S(2)}, u32[]{:S(2)}) collective-permute-start(bf16[2,6,2,128,128]{4,3,2,1,0:T(8,128)(2,1)} %get-tuple-element.7.d_ref), channel_id=1, source_target_pairs={{8,0},{10,2},{4,12},{6,14},{9,1},{11,3},{5,13},{7,15},{24,16},{26,... | collective-permute-start | bytes 2359304 | tf_op jit(solution)/shard_map/ppermute | solution.py:242
  19.0 5.2 %collective-permute-start = (s32[49]{0:T(128)S(1)}, s32[49]{0:T(128)S(1)}, u32[]{:S(2)}, u32[]{:S(2)}) collective-permute-start(s32[49]{0:T(128)S(1)} %pad_add_fusion), channel_id=1, source_target_pairs={{0,1},{1,0},{2,3},{3,2},{4,5},{5,4},{6,7},{7,6},{8,9},{9,8},{10,11... | collective-permute-start | bytes 596 | tf_op jit(solution)/shard_map/ppermute | solution.py:241
  19.3 111.6 %collective-permute-start.7 = (bf16[2,6,2,128,128]{4,3,2,1,0:T(8,128)(2,1)}, bf16[2,6,2,128,128]{4,3,2,1,0:T(8,128)(2,1)}, u32[]{:S(2)}, u32[]{:S(2)}) collective-permute-start(bf16[2,6,2,128,128]{4,3,2,1,0:T(8,128)(2,1)} %get-tuple-element.5), channel_id=1, source_target_pairs={{8,0},{10,2},{4,12},{6,14},{9,1},{11,3},{5,13},{7,15},{24,16},{26,... | collective-permute-start | bytes 2359304 | tf_op jit(solution)/shard_map/ppermute | solution.py:242
  21.5 105.0 %collective-permute-start.5 = (bf16[2,6,2,128,128]{4,3,2,1,0:T(8,128)(2,1)}, bf16[2,6,2,128,128]{4,3,2,1,0:T(8,128)(2,1)}, u32[]{:S(2)}, u32[]{:S(2)}) collective-permute-start(bf16[2,6,2,128,128]{4,3,2,1,0:T(8,128)(2,1)} %get-tuple-element.6), channel_id=1, source_target_pairs={{8,0},{10,2},{4,12},{6,14},{9,1},{11,3},{5,13},{7,15},{24,16},{26,... | collective-permute-start | bytes 2359304 | tf_op jit(solution)/shard_map/ppermute | solution.py:242
  24.3 44.3 %collective-permute-start.2 = (s32[98]{0:T(128)S(1)}, s32[98]{0:T(128)S(1)}, u32[]{:S(2)}, u32[]{:S(2)}) collective-permute-start(s32[98]{0:T(128)S(1)} %pad_add_fusion.2), channel_id=1, source_target_pairs={{8,0},{10,2},{4,12},{6,14},{9,1},{11,3},{5,13},{7,15},{24,16},{26,... | collective-permute-start | bytes 1184 | tf_op jit(solution)/shard_map/ppermute | solution.py:242
  68.6 53.5 %collective-permute-start.6 = (bf16[2,6,2,128,128]{4,3,2,1,0:T(8,128)(2,1)}, bf16[2,6,2,128,128]{4,3,2,1,0:T(8,128)(2,1)}, u32[]{:S(2)}, u32[]{:S(2)}) collective-permute-start(bf16[2,6,2,128,128]{4,3,2,1,0:T(8,128)(2,1)} %get-tuple-element.8), channel_id=1, source_target_pairs={{8,0},{10,2},{4,12},{6,14},{9,1},{11,3},{5,13},{7,15},{24,16},{26,... | collective-permute-start | bytes 2359304 | tf_op jit(solution)/shard_map/ppermute | solution.py:242
  74.8 21.6 %collective-permute-start.3 = (bf16[2,6,2,128,128]{4,3,2,1,0:T(8,128)(2,1)}, bf16[2,6,2,128,128]{4,3,2,1,0:T(8,128)(2,1)S(1)}, u32[]{:S(2)}, u32[]{:S(2)}) collective-permute-start(bf16[2,6,2,128,128]{4,3,2,1,0:T(8,128)(2,1)} %collective-permute-done.1.a_ref.field_ref), channel_id=1, source_target_pairs={{0,1},{1,0},{2,3},{3,2},{4,5},{5,4},{6,7},{7,6},{8,9},{9,8},{10,11... | collective-permute-start | bytes 2359304 | tf_op jit(solution)/shard_map/ppermute | solution.py:241
  93.7 2.7 %copy-start = (f32[4,6,2,2,128,128]{5,4,3,2,1,0:T(8,128)}, f32[4,6,2,2,128,128]{5,4,3,2,1,0:T(8,128)S(1)}, u32[]{:S(2)}) copy-start(f32[4,6,2,2,128,128]{5,4,3,2,1,0:T(8,128)S(1)} %weights.2.u0_ref.refs_4_) | copy-start | bytes 18874372
  115.0 2.6 %copy-start.1 = (f32[4,6,2,2,128,128]{5,4,3,2,1,0:T(8,128)}, f32[4,6,2,2,128,128]{5,4,3,2,1,0:T(8,128)S(1)}, u32[]{:S(2)}) copy-start(f32[4,6,2,2,128,128]{5,4,3,2,1,0:T(8,128)S(1)} %weights.3.u1_ref.refs_5_) | copy-start | bytes 18874372
  136.2 6.0 %collective-permute-start.10 = (f32[8,128]{1,0:T(8,128)}, f32[8,128]{1,0:T(8,128)S(1)}, u32[]{:S(2)}, u32[]{:S(2)}) collective-permute-start(f32[8,128]{1,0:T(8,128)} %last.1), channel_id=1, source_target_pairs={{0,9},{1,8},{2,11},{3,10},{12,5},{13,4},{14,7},{15,6},{16,25},{17,... | collective-permute-start | bytes 12296 | tf_op jit(solution)/shard_map/ppermute | solution.py:272
  137.5 6.7 %collective-permute-start.9 = (f32[8,128]{1,0:T(8,128)}, f32[8,128]{1,0:T(8,128)S(1)}, u32[]{:S(2)}, u32[]{:S(2)}) collective-permute-start(f32[8,128]{1,0:T(8,128)} %last.1), channel_id=1, source_target_pairs={{0,8},{1,9},{2,10},{3,11},{12,4},{13,5},{14,6},{15,7},{16,24},{17,... | collective-permute-start | bytes 12296 | tf_op jit(solution)/shard_map/ppermute | solution.py:272
  138.8 5.4 %collective-permute-start.8 = (f32[8,128]{1,0:T(8,128)}, f32[8,128]{1,0:T(8,128)S(1)}, u32[]{:S(2)}, u32[]{:S(2)}) collective-permute-start(f32[8,128]{1,0:T(8,128)} %last.1), channel_id=1, source_target_pairs={{0,1},{1,0},{2,3},{3,2},{4,5},{5,4},{6,7},{7,6},{8,9},{9,8},{10,11... | collective-permute-start | bytes 12296 | tf_op jit(solution)/shard_map/ppermute | solution.py:241

commit v2 on v0

v2 whole, which is shorter than its diff:
```python
import jax
import jax.numpy as jnp
from jax import lax
from jax.experimental import pallas as pl
from jax.experimental.pallas import tpu as pltpu
from jax.sharding import PartitionSpec as P

F32 = jnp.float32
BF16 = jnp.bfloat16
I32 = jnp.int32
SMEM = pl.BlockSpec(memory_space=pltpu.SMEM)
VMEM = pl.BlockSpec(memory_space=pltpu.VMEM)
ANY = pl.BlockSpec(memory_space=pl.ANY)


def one_way_pairs(count):
    half = count // 2
    outer = half // 2
    return [(g + half, g) if g < outer else (g, g + half) for g in range(half)]


def cost(flops, size):
    return pl.CostEstimate(flops=flops, bytes_accessed=size, transcendentals=0)


def pick_source_kernel(source_ref, fields_ref, out_ref, sem):
    time = lax.rem(source_ref[0], I32(fields_ref.shape[0]))
    copy = pltpu.make_async_copy(fields_ref.at[time], out_ref, sem)
    copy.start()
    copy.wait()


def pick_source(source, fields):
    return pl.pallas_call(
        pick_source_kernel,
        out_shape=jax.ShapeDtypeStruct(fields.shape[1:], fields.dtype),
        in_specs=[SMEM, ANY],
        out_specs=ANY,
        scratch_shapes=[pltpu.SemaphoreType.DMA],
        cost_estimate=cost(0, 1_600_000),
        compiler_params=pltpu.CompilerParams(vmem_limit_bytes=60 * 2**20),
        name="pick_source",
    )(source, fields)


def pick_kernel(order_ref, fields_ref, *refs):
    *outs, sems = refs
    copies = [
        pltpu.make_async_copy(fields_ref.at[order_ref[slot + 1]], out, sems.at[slot])
        for slot, out in enumerate(outs)
    ]
    for copy in copies:
        copy.start()
    for copy in copies:
        copy.wait()


def pick_others(order, fields):
    others = fields.shape[0] - 1
    return pl.pallas_call(
        pick_kernel,
        out_shape=[jax.ShapeDtypeStruct(fields.shape[1:], fields.dtype)] * others,
        in_specs=[SMEM, ANY],
        out_specs=[ANY] * others,
        scratch_shapes=[pltpu.SemaphoreType.DMA((others,))],
        cost_estimate=cost(0, others * 1_600_000),
        compiler_params=pltpu.CompilerParams(vmem_limit_bytes=60 * 2**20),
        name="pick_others",
    )(order, fields)


def plan_kernel(core_ref, own_ref, other_ref, deltas_ref, order_ref, sinks_ref):
    times = order_ref.shape[0]
    deltas = deltas_ref.shape[0]
    sinks = []
    for s, ref in enumerate((own_ref, other_ref)):
        for k in range(deltas):
            sink = lax.rem(ref[0] + deltas_ref[k], I32(2 * times))
            sinks_ref[s * deltas + k] = sink
            sinks.append(sink)
    base = core_ref[0] * times
    first = own_ref[0] - base
    keys = []
    for t in range(times):
        needed = sinks[0] == base + t
        for sink in sinks[1:]:
            needed = needed | (sink == base + t)
        key = jnp.where(needed, I32(t), I32(times + t))
        keys.append(jnp.where(first == t, I32(-1), key))
    for t in range(times):
        rank = I32(0)
        for other in range(times):
            if other != t:
                rank += (keys[other] < keys[t]).astype(I32)
        order_ref[rank] = I32(t)


def plan(core, own, other, deltas, times):
    return pl.pallas_call(
        plan_kernel,
        out_shape=[
            jax.ShapeDtypeStruct((times,), I32),
            jax.ShapeDtypeStruct((2 * deltas.shape[0],), I32),
        ],
        in_specs=[SMEM] * 4,
        out_specs=[SMEM] * 2,
        cost_estimate=cost(0, 1000),
        name="plan",
    )(core, own, other, deltas)


def weights_kernel(
    order_ref, far_ref, own_ref, far_cols, own_cols, m_cols, b_cols, a_ref, d_ref, b_ref, u_ref, la, ld, bs, yn
):
    slot = pl.program_id(0)
    rows, per_row, size = a_ref.shape[1], a_ref.shape[2], a_ref.shape[3]
    times = order_ref.shape[0]
    step = rows * per_row
    base = order_ref[slot] * step
    a_base = lax.rem(far_ref[0], I32(times)) * step
    d_base = lax.rem(own_ref[0], I32(times)) * step
    lo, hi = pl.ds(0, size), pl.ds(size, size)

    @pl.when(slot == 0)
    def _():
        for r in range(rows):
            for j in range(per_row):
                real, imag = a_ref[0, r, j], a_ref[1, r, j]
                la[r, j, lo, lo] = real
                la[r, j, lo, hi] = -imag
                la[r, j, hi, lo] = imag
                la[r, j, hi, hi] = real
                real, imag = d_ref[0, r, j].T, d_ref[1, r, j].T
                ld[r, j, lo, lo] = real
                ld[r, j, lo, hi] = -imag
                ld[r, j, hi, lo] = imag
                ld[r, j, hi, hi] = real

    for r in range(rows):
        for j in range(per_row):
            bs[r, lo, pl.ds(j * size, size)] = b_ref[0, 0, r, j]
            bs[r, hi, pl.ds(j * size, size)] = b_ref[0, 1, r, j]

    yn[...] = jnp.zeros_like(yn)
    for r in range(rows):
        inners = [far_cols[a_base + r * per_row + j] for j in range(per_row)]
        parts = [
            jnp.dot(la[r, j], bs[inners[j]], preferred_element_type=F32) for j in range(per_row)
        ]
        pieces = []
        for j in range(per_row):
            for k in range(per_row):
                col = b_cols[base + inners[j] * per_row + k]
                pieces.append((j, col, parts[j][:, k * size : (k + 1) * size]))
        for at in reversed(range(len(pieces))):
            j, col, value = pieces[at]
            for other_j, other_col, other in pieces:
                if other_j > j:
                    value = value + jnp.where(other_col == col, 1.0, 0.0) * other
            yn[col, pl.ds(r * size, size), lo] = value[:size].astype(BF16)
            yn[col, pl.ds(r * size, size), hi] = value[size:].astype(BF16)

    trace_real = jnp.zeros((size, size), F32)
    trace_imag = jnp.zeros((size, size), F32)
    for r in range(rows):
        trace_real += yn[r, pl.ds(r * size, size), lo].astype(F32)
        trace_imag += yn[r, pl.ds(r * size, size), hi].astype(F32)
    diagonal = lax.broadcasted_iota(I32, (size, size), 0) == lax.broadcasted_iota(I32, (size, size), 1)
    trace_real = jnp.sum(jnp.where(diagonal, trace_real, 0.0))
    trace_imag = jnp.sum(jnp.where(diagonal, trace_imag, 0.0))

    for r in range(rows):
        for j in range(per_row):
            col = m_cols[base + r * per_row + j]
            pick = I32(0)
            keep = F32(0)
            for k in range(per_row):
                hit = own_cols[d_base + col * per_row + k] == r
                pick = jnp.where(hit, I32(k), pick)
                keep = jnp.where(hit, F32(1), keep)
            real = ld[col, pick, lo, lo].astype(F32)
            imag = ld[col, pick, hi, lo].astype(F32)
            weight_real, weight_imag = trace_real * keep, trace_imag * keep
            u_ref[0, r, j, 0] = weight_real * real - weight_imag * imag
            u_ref[0, r, j, 1] = weight_real * imag + weight_imag * real

    for i in range(rows):
        for j in range(per_row):
            r = own_cols[d_base + i * per_row + j]
            met = [m_cols[base + r * per_row + k] for k in range(per_row)]
            right = jnp.concatenate(
                [yn[i, pl.ds(pl.multiple_of(col * size, size), size)] for col in met], axis=0
            )
            part = lax.dot_general(
                ld[i, j], right, (((1,), (1,)), ((), ())), preferred_element_type=F32
            )
            for k in range(per_row):
                u_ref[0, r, k, 0] -= part[:size, k * size : (k + 1) * size]
                u_ref[0, r, k, 1] -= part[size:, k * size : (k + 1) * size]


def weights(order, far_time, own_time, far_cols, own_cols, m_cols, b_cols, a, d, fields):
    times = fields.shape[0]
    _, rows, per_row, size, _ = a.shape
    whole = lambda slot, *_: (0, 0, 0, 0, 0)
    return pl.pallas_call(
        weights_kernel,
        out_shape=jax.ShapeDtypeStruct((times, rows, per_row, 2, size, size), F32),
        grid_spec=pltpu.PrefetchScalarGridSpec(
            num_scalar_prefetch=7,
            grid=(times,),
            in_specs=[
                pl.BlockSpec(a.shape, whole),
                pl.BlockSpec(a.shape, whole),
                pl.BlockSpec((1,) + a.shape, lambda slot, order, *_: (order[slot], 0, 0, 0, 0, 0)),
            ],
            out_specs=pl.BlockSpec(
                (1, rows, per_row, 2, size, size), lambda slot, *_: (slot, 0, 0, 0, 0, 0)
            ),
            scratch_shapes=[
                pltpu.VMEM((rows, per_row, 2 * size, 2 * size), BF16),
                pltpu.VMEM((rows, per_row, 2 * size, 2 * size), BF16),
                pltpu.VMEM((rows, 2 * size, per_row * size), BF16),
                pltpu.VMEM((rows, rows * size, 2 * size), BF16),
            ],
        ),
        compiler_params=pltpu.CompilerParams(vmem_limit_bytes=24 * 2**20),
        cost_estimate=cost(times * 20_000_000_000, times * 8_000_000),
        name="weights",
    )(order, far_time, own_time, far_cols, own_cols, m_cols, b_cols, a, d, fields)


def products(field_ref, u_refs, slot):
    _, rows, per_row, size, _ = field_ref.shape
    chunk = min(size, 32)
    fold = lambda x: jnp.sum(x.reshape(chunk // 8, 8, size), axis=0)
    sums = [jnp.zeros((8, size), F32) for _ in range(2 * len(u_refs))]
    for r in range(rows):
        for j in range(per_row):
            for start in range(0, size, chunk):
                at = pl.ds(start, chunk)
                real = field_ref[0, r, j, at].astype(F32)
                imag = field_ref[1, r, j, at].astype(F32)
                for s, u_ref in enumerate(u_refs):
                    u_real, u_imag = u_ref[slot, r, j, 0, at], u_ref[slot, r, j, 1, at]
                    sums[2 * s] += fold(real * u_real - imag * u_imag)
                    sums[2 * s + 1] += fold(real * u_imag + imag * u_real)
    return sums


def inner_kernel(slot, field_ref, u0_ref, u1_ref, out_ref):
    for at, value in enumerate(products(field_ref, (u0_ref, u1_ref), slot)):
        out_ref[at] = value


def inner(slot, field, u0, u1):
    return pl.pallas_call(
        lambda *refs: inner_kernel(slot, *refs),
        out_shape=jax.ShapeDtypeStruct((4, 8, field.shape[-1]), F32),
        in_specs=[VMEM] * 3,
        out_specs=VMEM,
        cost_estimate=cost(4_000_000, 4_000_000),
        compiler_params=pltpu.CompilerParams(vmem_limit_bytes=24 * 2**20),
        name="inner",
    )(field, u0, u1)


def last_kernel(core_ref, order_ref, sinks_ref, *refs):
    *earlier, field_ref, u0_ref, u1_ref, mine_ref, theirs_ref = refs
    slots = order_ref.shape[0]
    deltas = sinks_ref.shape[0] // 2
    share = deltas // 2
    core = core_ref[0]
    sums = [[ref[at] for at in range(4)] for ref in earlier]
    sums.append(products(field_ref, (u0_ref, u1_ref), slots - 1))
    for out_ref, owner in ((mine_ref, core), (theirs_ref, 1 - core)):
        lines = [jnp.zeros(sums[0][0].shape, F32) for _ in range(2 * share)]
        for slot in range(slots):
            time = core * slots + order_ref[slot]
            for s in range(2):
                for k in range(share):
                    sink = sinks_ref[s * deltas + owner * share + k]
                    keep = jnp.where(sink == time, F32(1), F32(0))
                    for part in range(2):
                        lines[part * share + k] += keep * sums[slot][2 * s + part]
        table = jnp.concatenate([jnp.sum(line, axis=0, keepdims=True) for line in lines], axis=0)
        table = jnp.sum(table, axis=1, keepdims=True)
        for part in range(2):
            out_ref[part] = table[part * share : (part + 1) * share]


def last(core, order, sinks, earlier, field, u0, u1):
    share = sinks.shape[0] // 4
    return pl.pallas_call(
        last_kernel,
        out_shape=[jax.ShapeDtypeStruct((2, share, 1), F32)] * 2,
        in_specs=[SMEM] * 3 + [VMEM] * (len(earlier) + 3),
        out_specs=[VMEM] * 2,
        cost_estimate=cost(4_000_000, 4_000_000),
        compiler_params=pltpu.CompilerParams(vmem_limit_bytes=24 * 2**20),
        name="last",
    )(core, order, sinks, *earlier, field, u0, u1)


def local(fields, block_cols, sources, deltas, partner):
    assert fields.shape[0] == 1 and lax.axis_size("src") == 2
    del partner
    fields = fields[0]
    times = fields.shape[0]
    core = lax.axis_index("src").reshape(1)
    pairs = one_way_pairs(lax.axis_size("mom"))
    swap = lambda value: lax.ppermute(value, "src", [(0, 1), (1, 0)])
    to_partner = lambda value: lax.ppermute(value, "mom", pairs)

    cols = block_cols.reshape(-1)
    far_cols = to_partner(cols)
    own_field = pick_source(sources, fields)
    far = [to_partner(own_field)]

    other_time = swap(sources)
    order, sinks = plan(core, sources, other_time, deltas, times)
    far += [to_partner(field) for field in pick_others(order, fields)]

    other_cols = swap(cols)
    far_other_cols = swap(far_cols)
    other_field = swap(own_field)
    far_other = swap(far[0])
    u0 = weights(order, sources, sources, far_cols, cols, far_cols, cols, far[0], own_field, fields)
    u1 = weights(
        order, other_time, other_time, far_other_cols, other_cols, far_cols, cols, far_other, other_field, fields
    )
    earlier = [inner(slot, far[slot], u0, u1) for slot in range(times - 1)]
    mine, theirs = last(core, order, sinks, earlier, far[-1], u0, u1)

    both = ("mom", "src")
    straight = [(2 * a + c, 2 * b + c) for b, a in pairs for c in range(2)]
    crossed = [(2 * a + c, 2 * b + 1 - c) for b, a in pairs for c in range(2)]
    return mine + swap(theirs) + lax.ppermute(mine, both, straight) + lax.ppermute(theirs, both, crossed)


def solution(mesh):
    in_specs = (
        P(("ens", "mom"), "src", None, None, None, None, None),
        P(("ens", "mom"), "src", None, None),
        P("src"),
        P(),
        P("mom"),
    )
    out_specs = P(None, "src", ("ens", "mom"))
    return jax.shard_map(local, mesh=mesh, in_specs=in_specs, out_specs=out_specs, check_vma=False)
```

time: 516 us -> 172 us (0.33)
  local copies, waits for them, and re-layouts: 171 us -> 3.3 us
  Pallas kernels: 0 us -> 128 us
  waiting for transfers between devices: 143 us -> 24.5 us
  matrix products: 83.4 us -> 0 us
  other arithmetic: 43.9 us -> 0.01 us
  loops' own time: 43.5 us -> 0 us
  between operations: 14.8 us -> 0.98 us
  starting transfers between devices: 6.18 us -> 15.4 us
  blocking collectives: 6.04 us -> 0 us
    pallas_call x0 -> x9, Pallas kernels: none -> 128 us  [the longest x1 73.3 us: pick_others(): pl.pallas_call(pick_kernel, out_shape=[jax.ShapeDtypeStruct(fields.shape[...]
    ppermute x2 -> x13, waiting for transfers between devices: 135 us -> 24.5 us  [the longest x5 19.3 us: local(): to_partner = lambda value: lax.ppermute(value, 'mom', pairs)]
    dot_general x40 -> x0, matrix products: 83.4 us -> none  [the longest x8 64.9 us: block_product(): jnp.einsum('rjkc,xrjkae->xrace', onehot, stacked, precision=lax.Precision...]
    transpose x8 -> x0, local copies, waits for them, and re-layouts: 49.8 us -> none  [pair_term(): second_flip = jnp.swapaxes(second_wide, 1, 2)]
    another operation x1 -> x0, loops' own time: 43.5 us -> none  [local(): lax.map(one_item, jnp.arange(slot_count * delta_count, dtype=jnp.int32))]
    slice x28 -> x0, local copies, waits for them, and re-layouts: 42.6 us -> none  [the longest x4 16.6 us: pair_term(): first_wide[1] * second_flip[1]]
    another operation x8 -> x0, local copies, waits for them, and re-layouts: 41.1 us -> none  [block_product(): stacked = jnp.stack([real_part, imag_part])]
    reduce_sum x4 -> x0, other arithmetic: 17.5 us -> none  [pair_term(): jnp.sum(first_wide[0] * second_flip[0] - first_wide[1] * second_flip[1])]
  transfers between devices with their start and end apart: 4 -> 13, of which waited for: 2 -> 4; matrix products, arithmetic and copies ran while one was open for 1% -> 1% of each run, Pallas kernels for 0% -> 59%
where the time goes in v2:
time: 172 us
  Pallas kernels  128 us (74%)
  waiting for transfers between devices  24.5 us (14%)
  starting transfers between devices  15.4 us (9%)
  local copies, waits for them, and re-layouts  3.3 us (2%)
    pallas_call x1, Pallas kernels, pick_others(): pl.pallas_call(pick_kernel, out_shape=[jax.ShapeDtypeStruct(fields.shape[...  73.3 us
    pallas_call x1, Pallas kernels, pick_source(): pl.pallas_call(pick_source_kernel, out_shape=jax.ShapeDtypeStruct(fields....  24.9 us
    pallas_call x2, Pallas kernels, weights(): pl.pallas_call(weights_kernel, out_shape=jax.ShapeDtypeStruct((times, row...  21.6 us
    ppermute x5, waiting for transfers between devices, local(): to_partner = lambda value: lax.ppermute(value, 'mom', pairs)  19.3 us
    ppermute x5, starting transfers between devices, local(): to_partner = lambda value: lax.ppermute(value, 'mom', pairs)  11.6 us
    pallas_call x3, Pallas kernels, inner(): pl.pallas_call(lambda *refs: inner_kernel(slot, *refs), out_shape=jax.Sha...  4.68 us
  transfers between devices with their start and end apart: 13, of which 4 were waited for; matrix products, arithmetic and copies ran while one was open for 1% of the time, Pallas kernels for 59%

profile of v2, /device:TPU:8, one launch (start us, length us, event | category | flops | bytes accessed | tf_op | source)
XLA Modules:
  0.0 171.7 jit_solution(14261770211310929609)
XLA Ops:
  0.0 0.0 copy-start
  0.8 24.9 %pick_source.1.d_ref = bf16[2,6,2,128,128]{4,3,2,1,0:T(8,128)(2,1)} custom-call(s32[1]{0:T(128)S(6)} %copy.9.own_ref.source_ref.far_ref, bf16[4,2,6,2,128,128]{5,4,3,2,1,0:T(8,128)(2,1)} %bitcast.2), custom_call_target="tpu_custom_call" | custom-call | bytes 1600000 | tf_op jit(solution)/shard_map/pick_source/pallas_call | solution.py:34
  25.7 5.4 %collective-permute-start.1 = (bf16[2,6,2,128,128]{4,3,2,1,0:T(8,128)(2,1)}, bf16[2,6,2,128,128]{4,3,2,1,0:T(8,128)(2,1)}, u32[]{:S(2)}, u32[]{:S(2)}) collective-permute-start(bf16[2,6,2,128,128]{4,3,2,1,0:T(8,128)(2,1)} %pick_source.1.d_ref), channel_id=1, source_target_pairs={{8,0},{10,2},{4,12},{6,14},{9,1},{11,3},{5,13},{7,15},{24,16},{26,... | collective-permute-start | bytes 2359304 | tf_op jit(solution)/shard_map/ppermute | solution.py:313
  31.1 0.0 collective-permute-start
  31.1 0.8 copy.7
  31.9 0.1 reshape.7.own_cols.b_cols
  32.0 1.3 collective-permute-start.2
  33.3 0.6 collective-permute-start.4
  33.9 0.1 collective-permute-start.6
  34.0 0.0 collective-permute-done.other_ref.far_ref.own_ref
  34.0 1.9 %plan.1 = (s32[4]{0:T(128)}, s32[8]{0:T(128)}) custom-call(s32[1]{0:T(128)} %bitcast.core_ref, s32[1]{0:T(128)S(6)} %copy.9.own_ref.source_ref.far_ref, s32[1]{0:T(128)} %collective-permute-done.other_ref.far_ref.own_ref, s32[4]{0:T(128)} %deltas_ref.1), custom_call_target="tpu_custom_call" | custom-call | bytes 1000 | tf_op jit(solution)/shard_map/plan/pallas_call | solution.py:99
  35.9 73.3 %pick_others.1 = (bf16[2,6,2,128,128]{4,3,2,1,0:T(8,128)(2,1)}, bf16[2,6,2,128,128]{4,3,2,1,0:T(8,128)(2,1)}, bf16[2,6,2,128,128]{4,3,2,1,0:T(8,128)(2,1)}) custom-call(s32[4]{0:T(128)} %get-tuple-element.12.order_ref, bf16[4,2,6,2,128,128]{5,4,3,2,1,0:T(8,128)(2,1)} %bitcast.3), custom_call_target="tpu_custom_call" | custom-call | bytes 4800000 | tf_op jit(solution)/shard_map/pick_others/pallas_call | solution.py:60
  109.2 0.0 copy-start.3
  109.2 2.2 %collective-permute-start.7 = (bf16[2,6,2,128,128]{4,3,2,1,0:T(8,128)(2,1)}, bf16[2,6,2,128,128]{4,3,2,1,0:T(8,128)(2,1)}, u32[]{:S(2)}, u32[]{:S(2)}) collective-permute-start(bf16[2,6,2,128,128]{4,3,2,1,0:T(8,128)(2,1)} %get-tuple-element.14), channel_id=1, source_target_pairs={{8,0},{10,2},{4,12},{6,14},{9,1},{11,3},{5,13},{7,15},{24,16},{26,... | collective-permute-start | bytes 2359304 | tf_op jit(solution)/shard_map/ppermute | solution.py:313
  111.4 0.0 collective-permute-done.2.far_cols.m_cols
  111.4 0.4 collective-permute-start.3
  111.8 0.0 collective-permute-done.1.a_ref.refs_0_
  111.8 0.1 collective-permute-start.5
  111.9 0.0 copy-done
  111.9 0.0 copy-start.1
  111.9 1.1 copy-done.1
  113.1 0.6 copy-done.2
  113.7 10.1 %weights.2.refs_1_.refs_4_ = f32[4,6,2,2,128,128]{5,4,3,2,1,0:T(8,128)S(1)} custom-call(s32[4]{0:T(128)S(1)} %copy-done.2, s32[1]{0:T(128)S(6)} %copy.9.own_ref.source_ref.far_ref, s32[1]{0:T(128)S(6)} %copy.9.own_ref.source_ref.far_ref, s32[48]{0:T(128)S(1)} %collective-permute-done.2.far_cols.m_cols, s32[48]{0:T(128)S(1)} %reshape.7.own_cols.b_cols, ...), custom_call_target="tpu_custom_call" | custom-call | flops 80000000000 | bytes 32000000 | tf_op jit(solution)/shard_map/weights/pallas_call | solution.py:206
  123.8 0.0 collective-permute-done.4.own_cols
  123.8 0.0 copy-done.6
  123.8 1.3 collective-permute-start.8
  125.1 0.0 collective-permute-done.3.far_cols
  125.1 0.0 copy-done.5
  125.2 1.3 collective-permute-start.9
  126.5 0.0 collective-permute-done.6.d_ref
  126.5 0.0 collective-permute-done.5.a_ref
  126.5 0.0 copy-done.3
  126.5 11.5 %weights.3.refs_2_.refs_5_ = f32[4,6,2,2,128,128]{5,4,3,2,1,0:T(8,128)S(1)} custom-call(s32[4]{0:T(128)S(1)} %copy-done.3, s32[1]{0:T(128)} %collective-permute-done.other_ref.far_ref.own_ref, s32[1]{0:T(128)} %collective-permute-done.other_ref.far_ref.own_ref, s32[48]{0:T(128)S(1)} %collective-permute-done.3.far_cols, ...), custom_call_target="tpu_custom_call" | custom-call | flops 80000000000 | bytes 32000000 | tf_op jit(solution)/shard_map/weights/pallas_call | solution.py:206
  138.1 1.9 %inner.3.refs_0_ = f32[4,8,128]{2,1,0:T(8,128)S(1)} custom-call(bf16[2,6,2,128,128]{4,3,2,1,0:T(8,128)(2,1)} %collective-permute-done.1.a_ref.refs_0_, f32[4,6,2,2,128,128]{5,4,3,2,1,0:T(8,128)S(1)} %weights.2.refs_1_.refs_4_, f32[4,6,2,2,128,128]{5,4,3,2,1,0:T(8,128)S(1)} %weights.3.refs_2_.refs_5_), custom_call_target="tpu_custom_call" | custom-call | flops 4000000 | bytes 4000000 | tf_op jit(solution)/shard_map/inner/pallas_call | solution.py:257
  140.0 0.0 collective-permute-done.7.refs_0_
  140.0 1.9 %inner.4.refs_1_ = f32[4,8,128]{2,1,0:T(8,128)S(1)} custom-call(bf16[2,6,2,128,128]{4,3,2,1,0:T(8,128)(2,1)} %collective-permute-done.7.refs_0_, f32[4,6,2,2,128,128]{5,4,3,2,1,0:T(8,128)S(1)} %weights.2.refs_1_.refs_4_, f32[4,6,2,2,128,128]{5,4,3,2,1,0:T(8,128)S(1)} %weights.3.refs_2_.refs_5_), custom_call_target="tpu_custom_call" | custom-call | flops 4000000 | bytes 4000000 | tf_op jit(solution)/shard_map/inner/pallas_call | solution.py:257
  141.9 3.6 %collective-permute-done.8.refs_0_ = bf16[2,6,2,128,128]{4,3,2,1,0:T(8,128)(2,1)S(1)} collective-permute-done((bf16[2,6,2,128,128]{4,3,2,1,0:T(8,128)(2,1)S(1)}, bf16[2,6,2,128,128]{4,3,2,1,0:T(8,128)(2,1)S(1)}, u32[]{:S(2)}, u32[]{:S(2)}) %collective-permute-start.8) | collective-permute-done | bytes 786464 | tf_op jit(solution)/shard_map/ppermute | solution.py:313
  145.5 0.9 inner.5.refs_2_
  146.4 15.7 %collective-permute-done.9.refs_3_ = bf16[2,6,2,128,128]{4,3,2,1,0:T(8,128)(2,1)S(1)} collective-permute-done((bf16[2,6,2,128,128]{4,3,2,1,0:T(8,128)(2,1)S(1)}, bf16[2,6,2,128,128]{4,3,2,1,0:T(8,128)(2,1)S(1)}, u32[]{:S(2)}, u32[]{:S(2)}) %collective-permute-start.9) | collective-permute-done | bytes 786464 | tf_op jit(solution)/shard_map/ppermute | solution.py:313
  162.1 0.0 copy-done.4
  162.1 1.1 last.1
  163.2 1.3 collective-permute-start.12
  164.5 0.1 collective-permute-start.10
  164.6 1.3 collective-permute-start.11
  165.9 3.1 %collective-permute-done.12 = f32[2,2,1]{2,1,0:T(2,128)S(1)} collective-permute-done((f32[2,2,1]{2,1,0:T(2,128)S(1)}, f32[2,2,1]{2,1,0:T(2,128)S(1)}, u32[]{:S(2)}, u32[]{:S(2)}) %collective-permute-start.12) | collective-permute-done | bytes 48 | tf_op jit(solution)/shard_map/ppermute | solution.py:338
  169.0 2.0 %collective-permute-done.11 = f32[2,2,1]{2,1,0:T(2,128)S(1)} collective-permute-done((f32[2,2,1]{2,1,0:T(2,128)S(1)}, f32[2,2,1]{2,1,0:T(2,128)S(1)}, u32[]{:S(2)}, u32[]{:S(2)}) %collective-permute-start.11) | collective-permute-done | bytes 48 | tf_op jit(solution)/shard_map/ppermute | solution.py:338
  171.0 0.0 collective-permute-done.10
  171.0 0.7 copy.8
  (5 shorter events, 0.0 us)
Async XLA Ops:
  0.0 111.9 %copy-start = (bf16[1,4,2,6,2,128,128]{6,5,4,3,2,1,0:T(8,128)(2,1)S(1)}, bf16[1,4,2,6,2,128,128]{6,5,4,3,2,1,0:T(8,128)(2,1)}, u32[]{:S(2)}) copy-start(bf16[1,4,2,6,2,128,128]{6,5,4,3,2,1,0:T(8,128)(2,1)} %param.5) | copy-start | bytes 9437188
  25.7 86.1 %collective-permute-start.1 = (bf16[2,6,2,128,128]{4,3,2,1,0:T(8,128)(2,1)}, bf16[2,6,2,128,128]{4,3,2,1,0:T(8,128)(2,1)}, u32[]{:S(2)}, u32[]{:S(2)}) collective-permute-start(bf16[2,6,2,128,128]{4,3,2,1,0:T(8,128)(2,1)} %pick_source.1.d_ref), channel_id=1, source_target_pairs={{8,0},{10,2},{4,12},{6,14},{9,1},{11,3},{5,13},{7,15},{24,16},{26,... | collective-permute-start | bytes 2359304 | tf_op jit(solution)/shard_map/ppermute | solution.py:313
  31.1 2.8 %collective-permute-start = (s32[1]{0:T(128)}, s32[1]{0:T(128)}, u32[]{:S(2)}, u32[]{:S(2)}) collective-permute-start(s32[1]{0:T(128)} %param.7), channel_id=1, source_target_pairs={{0,1},{1,0},{2,3},{3,2},{4,5},{5,4},{6,7},{7,6},{8,9},{9,8},{10,11... | collective-permute-start | bytes 20 | tf_op jit(solution)/shard_map/ppermute | solution.py:312
  32.0 79.4 %collective-permute-start.2 = (s32[48]{0:T(128)S(1)}, s32[48]{0:T(128)S(1)}, u32[]{:S(2)}, u32[]{:S(2)}) collective-permute-start(s32[48]{0:T(128)S(1)} %reshape.7.own_cols.b_cols), channel_id=1, source_target_pairs={{8,0},{10,2},{4,12},{6,14},{9,1},{11,3},{5,13},{7,15},{24,16},{26,... | collective-permute-start | bytes 584 | tf_op jit(solution)/shard_map/ppermute | solution.py:313
  33.3 90.4 %collective-permute-start.4 = (s32[48]{0:T(128)S(1)}, s32[48]{0:T(128)S(1)}, u32[]{:S(2)}, u32[]{:S(2)}) collective-permute-start(s32[48]{0:T(128)S(1)} %reshape.7.own_cols.b_cols), channel_id=1, source_target_pairs={{0,1},{1,0},{2,3},{3,2},{4,5},{5,4},{6,7},{7,6},{8,9},{9,8},{10,11... | collective-permute-start | bytes 584 | tf_op jit(solution)/shard_map/ppermute | solution.py:312
  33.9 92.6 %collective-permute-start.6 = (bf16[2,6,2,128,128]{4,3,2,1,0:T(8,128)(2,1)}, bf16[2,6,2,128,128]{4,3,2,1,0:T(8,128)(2,1)}, u32[]{:S(2)}, u32[]{:S(2)}) collective-permute-start(bf16[2,6,2,128,128]{4,3,2,1,0:T(8,128)(2,1)} %pick_source.1.d_ref), channel_id=1, source_target_pairs={{0,1},{1,0},{2,3},{3,2},{4,5},{5,4},{6,7},{7,6},{8,9},{9,8},{10,11... | collective-permute-start | bytes 2359304 | tf_op jit(solution)/shard_map/ppermute | solution.py:312
  109.2 17.3 %copy-start.3 = (s32[4]{0:T(128)S(1)}, s32[4]{0:T(128)}, u32[]{:S(2)}) copy-start(s32[4]{0:T(128)} %get-tuple-element.12.order_ref) | copy-start | bytes 52
  109.2 30.8 %collective-permute-start.7 = (bf16[2,6,2,128,128]{4,3,2,1,0:T(8,128)(2,1)}, bf16[2,6,2,128,128]{4,3,2,1,0:T(8,128)(2,1)}, u32[]{:S(2)}, u32[]{:S(2)}) collective-permute-start(bf16[2,6,2,128,128]{4,3,2,1,0:T(8,128)(2,1)} %get-tuple-element.14), channel_id=1, source_target_pairs={{8,0},{10,2},{4,12},{6,14},{9,1},{11,3},{5,13},{7,15},{24,16},{26,... | collective-permute-start | bytes 2359304 | tf_op jit(solution)/shard_map/ppermute | solution.py:313
  111.4 13.7 %collective-permute-start.3 = (s32[48]{0:T(128)S(1)}, s32[48]{0:T(128)S(1)}, u32[]{:S(2)}, u32[]{:S(2)}) collective-permute-start(s32[48]{0:T(128)S(1)} %collective-permute-done.2.far_cols.m_cols), channel_id=1, source_target_pairs={{0,1},{1,0},{2,3},{3,2},{4,5},{5,4},{6,7},{7,6},{8,9},{9,8},{10,11... | collective-permute-start | bytes 584 | tf_op jit(solution)/shard_map/ppermute | solution.py:312
  111.8 14.7 %collective-permute-start.5 = (bf16[2,6,2,128,128]{4,3,2,1,0:T(8,128)(2,1)}, bf16[2,6,2,128,128]{4,3,2,1,0:T(8,128)(2,1)S(1)}, u32[]{:S(2)}, u32[]{:S(2)}) collective-permute-start(bf16[2,6,2,128,128]{4,3,2,1,0:T(8,128)(2,1)} %collective-permute-done.1.a_ref.refs_0_), channel_id=1, source_target_pairs={{0,1},{1,0},{2,3},{3,2},{4,5},{5,4},{6,7},{7,6},{8,9},{9,8},{10,11... | collective-permute-start | bytes 2359304 | tf_op jit(solution)/shard_map/ppermute | solution.py:312
  111.9 1.1 copy-start.1
  113.1 0.6 copy-start.2
  113.7 10.1 %copy-start.6 = (bf16[2,6,2,128,128]{4,3,2,1,0:T(8,128)(2,1)S(1)}, bf16[2,6,2,128,128]{4,3,2,1,0:T(8,128)(2,1)}, u32[]{:S(2)}) copy-start(bf16[2,6,2,128,128]{4,3,2,1,0:T(8,128)(2,1)} %get-tuple-element.15) | copy-start | bytes 2359300
  113.7 11.5 %copy-start.5 = (bf16[2,6,2,128,128]{4,3,2,1,0:T(8,128)(2,1)S(1)}, bf16[2,6,2,128,128]{4,3,2,1,0:T(8,128)(2,1)}, u32[]{:S(2)}) copy-start(bf16[2,6,2,128,128]{4,3,2,1,0:T(8,128)(2,1)} %get-tuple-element.16) | copy-start | bytes 2359300
  123.8 21.7 %collective-permute-start.8 = (bf16[2,6,2,128,128]{4,3,2,1,0:T(8,128)(2,1)S(1)}, bf16[2,6,2,128,128]{4,3,2,1,0:T(8,128)(2,1)S(1)}, u32[]{:S(2)}, u32[]{:S(2)}) collective-permute-start(bf16[2,6,2,128,128]{4,3,2,1,0:T(8,128)(2,1)S(1)} %copy-done.6), channel_id=1, source_target_pairs={{8,0},{10,2},{4,12},{6,14},{9,1},{11,3},{5,13},{7,15},{24,16},{26,... | collective-permute-start | bytes 2359304 | tf_op jit(solution)/shard_map/ppermute | solution.py:313
  125.2 36.9 %collective-permute-start.9 = (bf16[2,6,2,128,128]{4,3,2,1,0:T(8,128)(2,1)S(1)}, bf16[2,6,2,128,128]{4,3,2,1,0:T(8,128)(2,1)S(1)}, u32[]{:S(2)}, u32[]{:S(2)}) collective-permute-start(bf16[2,6,2,128,128]{4,3,2,1,0:T(8,128)(2,1)S(1)} %copy-done.5), channel_id=1, source_target_pairs={{8,0},{10,2},{4,12},{6,14},{9,1},{11,3},{5,13},{7,15},{24,16},{26,... | collective-permute-start | bytes 2359304 | tf_op jit(solution)/shard_map/ppermute | solution.py:313
  141.9 20.2 %copy-start.4 = (s32[8]{0:T(128)S(1)}, s32[8]{0:T(128)}, u32[]{:S(2)}) copy-start(s32[8]{0:T(128)} %get-tuple-element.13.sinks_ref) | copy-start | bytes 100
  163.2 5.8 %collective-permute-start.12 = (f32[2,2,1]{2,1,0:T(2,128)S(1)}, f32[2,2,1]{2,1,0:T(2,128)S(1)}, u32[]{:S(2)}, u32[]{:S(2)}) collective-permute-start(f32[2,2,1]{2,1,0:T(2,128)S(1)} %get-tuple-element.18), channel_id=1, source_target_pairs={{0,9},{1,8},{2,11},{3,10},{12,5},{13,4},{14,7},{15,6},{16,25},{17,... | collective-permute-start | bytes 56 | tf_op jit(solution)/shard_map/ppermute | solution.py:338
  164.5 6.5 %collective-permute-start.10 = (f32[2,2,1]{2,1,0:T(2,128)S(1)}, f32[2,2,1]{2,1,0:T(2,128)S(1)}, u32[]{:S(2)}, u32[]{:S(2)}) collective-permute-start(f32[2,2,1]{2,1,0:T(2,128)S(1)} %get-tuple-element.18), channel_id=1, source_target_pairs={{0,1},{1,0},{2,3},{3,2},{4,5},{5,4},{6,7},{7,6},{8,9},{9,8},{10,11... | collective-permute-start | bytes 56 | tf_op jit(solution)/shard_map/ppermute | solution.py:312
  164.6 6.5 %collective-permute-start.11 = (f32[2,2,1]{2,1,0:T(2,128)S(1)}, f32[2,2,1]{2,1,0:T(2,128)S(1)}, u32[]{:S(2)}, u32[]{:S(2)}) collective-permute-start(f32[2,2,1]{2,1,0:T(2,128)S(1)} %get-tuple-element.17), channel_id=1, source_target_pairs={{0,8},{1,9},{2,10},{3,11},{12,4},{13,5},{14,6},{15,7},{16,24},{17,... | collective-permute-start | bytes 56 | tf_op jit(solution)/shard_map/ppermute | solution.py:338

commit v3 on v2

--- a/solution.py
+++ b/solution.py
@@ -35,10 +35,10 @@
         pick_source_kernel,
         out_shape=jax.ShapeDtypeStruct(fields.shape[1:], fields.dtype),
         in_specs=[SMEM, ANY],
-        out_specs=ANY,
+        out_specs=VMEM,
         scratch_shapes=[pltpu.SemaphoreType.DMA],
         cost_estimate=cost(0, 1_600_000),
-        compiler_params=pltpu.CompilerParams(vmem_limit_bytes=60 * 2**20),
+        compiler_params=pltpu.CompilerParams(vmem_limit_bytes=56 * 2**20),
         name="pick_source",
     )(source, fields)
 
@@ -61,10 +61,10 @@
         pick_kernel,
         out_shape=[jax.ShapeDtypeStruct(fields.shape[1:], fields.dtype)] * others,
         in_specs=[SMEM, ANY],
-        out_specs=[ANY] * others,
+        out_specs=[VMEM] * others,
         scratch_shapes=[pltpu.SemaphoreType.DMA((others,))],
         cost_estimate=cost(0, others * 1_600_000),
-        compiler_params=pltpu.CompilerParams(vmem_limit_bytes=60 * 2**20),
+        compiler_params=pltpu.CompilerParams(vmem_limit_bytes=24 * 2**20),
         name="pick_others",
     )(order, fields)
 

time: 172 us -> 85.6 us (0.50)
  Pallas kernels: 128 us -> 28.3 us
  waiting for transfers between devices: 24.5 us -> 31.3 us
  starting transfers between devices: 15.4 us -> 18.9 us
  local copies, waits for them, and re-layouts: 3.3 us -> 5.79 us
    pallas_call x1, Pallas kernels: 73.3 us -> 1.65 us  [pick_others(): pl.pallas_call(pick_kernel, out_shape=[jax.ShapeDtypeStruct(fields.shape[...]
    pallas_call x1, Pallas kernels: 24.9 us -> 2.04 us  [pick_source(): pl.pallas_call(pick_source_kernel, out_shape=jax.ShapeDtypeStruct(fields....]
    ppermute x5, waiting for transfers between devices: 19.3 us -> 26.1 us  [local(): to_partner = lambda value: lax.ppermute(value, 'mom', pairs)]
    ppermute x5, starting transfers between devices: 11.6 us -> 15 us  [local(): to_partner = lambda value: lax.ppermute(value, 'mom', pairs)]
    pallas_call x2, Pallas kernels: 21.6 us -> 18.8 us  [weights(): pl.pallas_call(weights_kernel, out_shape=jax.ShapeDtypeStruct((times, row...]
    unnamed x15, local copies, waits for them, and re-layouts: 2.55 us -> 5.04 us
    pallas_call x3, Pallas kernels: 4.68 us -> 2.78 us  [inner(): pl.pallas_call(lambda *refs: inner_kernel(slot, *refs), out_shape=jax.Sha...]
  transfers between devices with their start and end apart: 13 -> 13, of which waited for: 4 -> 5; matrix products, arithmetic and copies ran while one was open for 1% -> 1% of each run, Pallas kernels for 59% -> 30%
where the time goes in v3:
time: 85.6 us; the launch traced here: 85.1 us
  waiting for transfers between devices  31.3 us (37%)
  Pallas kernels  28.3 us (33%)
  starting transfers between devices  18.9 us (22%)
  local copies, waits for them, and re-layouts  5.79 us (7%)
  between operations  0.87 us (1%)
    ppermute x5, waiting for transfers between devices, local(): to_partner = lambda value: lax.ppermute(value, 'mom', pairs)  26.1 us
    pallas_call x2, Pallas kernels, weights(): pl.pallas_call(weights_kernel, out_shape=jax.ShapeDtypeStruct((times, row...  18.8 us
    ppermute x5, starting transfers between devices, local(): to_partner = lambda value: lax.ppermute(value, 'mom', pairs)  15 us
    unnamed x15, local copies, waits for them, and re-layouts  5.04 us
    ppermute x1, waiting for transfers between devices, local(): lax.ppermute(theirs, both, crossed)  3.12 us
    pallas_call x3, Pallas kernels, inner(): pl.pallas_call(lambda *refs: inner_kernel(slot, *refs), out_shape=jax.Sha...  2.78 us
    ppermute x1, waiting for transfers between devices, local(): lax.ppermute(mine, both, straight)  2.04 us
    pallas_call x1, Pallas kernels, pick_source(): pl.pallas_call(pick_source_kernel, out_shape=jax.ShapeDtypeStruct(fields....  2.04 us
  transfers between devices with their start and end apart: 13, of which 5 were waited for; matrix products, arithmetic and copies ran while one was open for 1% of the time, Pallas kernels for 30%

profile of v3, /device:TPU:8, one launch (start us, length us, event | category | flops | bytes accessed | tf_op | source)
XLA Modules:
  0.0 85.1 jit_solution(3170367271571487128)
XLA Ops:
  0.7 2.0 %pick_source.1.d_ref = bf16[2,6,2,128,128]{4,3,2,1,0:T(8,128)(2,1)} custom-call(s32[1]{0:T(128)S(6)} %copy.9.own_ref.source_ref.far_ref, bf16[4,2,6,2,128,128]{5,4,3,2,1,0:T(8,128)(2,1)} %bitcast.2), custom_call_target="tpu_custom_call" | custom-call | bytes 1600000 | tf_op jit(solution)/shard_map/pick_source/pallas_call | solution.py:34
  2.7 4.5 %collective-permute-start.1 = (bf16[2,6,2,128,128]{4,3,2,1,0:T(8,128)(2,1)}, bf16[2,6,2,128,128]{4,3,2,1,0:T(8,128)(2,1)S(1)}, u32[]{:S(2)}, u32[]{:S(2)}) collective-permute-start(bf16[2,6,2,128,128]{4,3,2,1,0:T(8,128)(2,1)} %pick_source.1.d_ref), channel_id=1, source_target_pairs={{8,0},{10,2},{4,12},{6,14},{9,1},{11,3},{5,13},{7,15},{24,16},{26,... | collective-permute-start | bytes 2359304 | tf_op jit(solution)/shard_map/ppermute | solution.py:313
  7.2 0.1 collective-permute-start
  7.3 0.8 copy.7
  8.1 0.1 reshape.7.own_cols.b_cols
  8.2 1.3 %collective-permute-start.2 = (s32[48]{0:T(128)S(1)}, s32[48]{0:T(128)S(1)}, u32[]{:S(2)}, u32[]{:S(2)}) collective-permute-start(s32[48]{0:T(128)S(1)} %reshape.7.own_cols.b_cols), channel_id=1, source_target_pairs={{8,0},{10,2},{4,12},{6,14},{9,1},{11,3},{5,13},{7,15},{24,16},{26,... | collective-permute-start | bytes 584 | tf_op jit(solution)/shard_map/ppermute | solution.py:313
  9.5 0.6 collective-permute-start.4
  10.1 0.1 collective-permute-start.6
  10.2 0.0 collective-permute-done.other_ref.far_ref.own_ref
  10.2 1.9 %plan.1 = (s32[4]{0:T(128)}, s32[8]{0:T(128)}) custom-call(s32[1]{0:T(128)} %bitcast.core_ref, s32[1]{0:T(128)S(6)} %copy.9.own_ref.source_ref.far_ref, s32[1]{0:T(128)} %collective-permute-done.other_ref.far_ref.own_ref, s32[4]{0:T(128)} %deltas_ref.1), custom_call_target="tpu_custom_call" | custom-call | bytes 1000 | tf_op jit(solution)/shard_map/plan/pallas_call | solution.py:99
  12.1 0.0 copy-start
  12.1 1.9 %copy-done = bf16[1,4,2,6,2,128,128]{6,5,4,3,2,1,0:T(8,128)(2,1)S(1)} copy-done((bf16[1,4,2,6,2,128,128]{6,5,4,3,2,1,0:T(8,128)(2,1)S(1)}, bf16[1,4,2,6,2,128,128]{6,5,4,3,2,1,0:T(8,128)(2,1)}, u32[]{:S(2)}) %copy-start) | copy-done | bytes 3145752
  14.0 0.6 copy-done.3
  14.6 1.6 %pick_others.1 = (bf16[2,6,2,128,128]{4,3,2,1,0:T(8,128)(2,1)}, bf16[2,6,2,128,128]{4,3,2,1,0:T(8,128)(2,1)S(1)}, bf16[2,6,2,128,128]{4,3,2,1,0:T(8,128)(2,1)S(1)}) custom-call(s32[4]{0:T(128)S(1)} %copy-done.3, bf16[4,2,6,2,128,128]{5,4,3,2,1,0:T(8,128)(2,1)S(1)} %bitcast.3), custom_call_target="tpu_custom_call" | custom-call | bytes 4800000 | tf_op jit(solution)/shard_map/pick_others/pallas_call | solution.py:60
  16.2 0.0 copy-start.5
  16.2 0.0 copy-start.1
  16.3 2.5 %collective-permute-start.7 = (bf16[2,6,2,128,128]{4,3,2,1,0:T(8,128)(2,1)}, bf16[2,6,2,128,128]{4,3,2,1,0:T(8,128)(2,1)}, u32[]{:S(2)}, u32[]{:S(2)}) collective-permute-start(bf16[2,6,2,128,128]{4,3,2,1,0:T(8,128)(2,1)} %get-tuple-element.14), channel_id=1, source_target_pairs={{8,0},{10,2},{4,12},{6,14},{9,1},{11,3},{5,13},{7,15},{24,16},{26,... | collective-permute-start | bytes 2359304 | tf_op jit(solution)/shard_map/ppermute | solution.py:313
  18.8 6.6 %collective-permute-done.2.far_cols.m_cols = s32[48]{0:T(128)S(1)} collective-permute-done((s32[48]{0:T(128)S(1)}, s32[48]{0:T(128)S(1)}, u32[]{:S(2)}, u32[]{:S(2)}) %collective-permute-start.2) | collective-permute-done | bytes 224 | tf_op jit(solution)/shard_map/ppermute | solution.py:313
  25.4 0.0 collective-permute-start.3
  25.4 0.0 collective-permute-done.1.a_ref.refs_0_
  25.4 0.5 collective-permute-start.5
  26.0 1.1 %copy-done.2 = bf16[2,6,2,128,128]{4,3,2,1,0:T(8,128)(2,1)S(1)} copy-done((bf16[2,6,2,128,128]{4,3,2,1,0:T(8,128)(2,1)S(1)}, bf16[2,6,2,128,128]{4,3,2,1,0:T(8,128)(2,1)}, u32[]{:S(2)}) %copy-start.2) | copy-done | bytes 786456
  27.1 0.6 copy-done.4
  27.7 8.7 %weights.2.refs_1_.refs_4_ = f32[4,6,2,2,128,128]{5,4,3,2,1,0:T(8,128)S(1)} custom-call(s32[4]{0:T(128)S(1)} %copy-done.4, s32[1]{0:T(128)S(6)} %copy.9.own_ref.source_ref.far_ref, s32[1]{0:T(128)S(6)} %copy.9.own_ref.source_ref.far_ref, s32[48]{0:T(128)S(1)} %collective-permute-done.2.far_cols.m_cols, s32[48]{0:T(128)S(1)} %reshape.7.own_cols.b_cols, ...), custom_call_target="tpu_custom_call" | custom-call | flops 80000000000 | bytes 32000000 | tf_op jit(solution)/shard_map/weights/pallas_call | solution.py:206
  36.4 0.0 collective-permute-done.4.own_cols
  36.4 5.3 %collective-permute-start.8 = (bf16[2,6,2,128,128]{4,3,2,1,0:T(8,128)(2,1)S(1)}, bf16[2,6,2,128,128]{4,3,2,1,0:T(8,128)(2,1)S(1)}, u32[]{:S(2)}, u32[]{:S(2)}) collective-permute-start(bf16[2,6,2,128,128]{4,3,2,1,0:T(8,128)(2,1)S(1)} %get-tuple-element.15), channel_id=1, source_target_pairs={{8,0},{10,2},{4,12},{6,14},{9,1},{11,3},{5,13},{7,15},{24,16},{26,... | collective-permute-start | bytes 2359304 | tf_op jit(solution)/shard_map/ppermute | solution.py:313
  41.7 0.0 collective-permute-done.3.far_cols
  41.8 1.3 %collective-permute-start.9 = (bf16[2,6,2,128,128]{4,3,2,1,0:T(8,128)(2,1)S(1)}, bf16[2,6,2,128,128]{4,3,2,1,0:T(8,128)(2,1)S(1)}, u32[]{:S(2)}, u32[]{:S(2)}) collective-permute-start(bf16[2,6,2,128,128]{4,3,2,1,0:T(8,128)(2,1)S(1)} %get-tuple-element.16), channel_id=1, source_target_pairs={{8,0},{10,2},{4,12},{6,14},{9,1},{11,3},{5,13},{7,15},{24,16},{26,... | collective-permute-start | bytes 2359304 | tf_op jit(solution)/shard_map/ppermute | solution.py:313
  43.1 0.0 collective-permute-done.6.d_ref
  43.1 0.0 collective-permute-done.5.a_ref
  43.1 0.0 copy-done.5
  43.1 0.0 copy-done.1
  43.1 10.1 %weights.3.refs_2_.refs_5_ = f32[4,6,2,2,128,128]{5,4,3,2,1,0:T(8,128)S(1)} custom-call(s32[4]{0:T(128)S(1)} %copy-done.5, s32[1]{0:T(128)} %collective-permute-done.other_ref.far_ref.own_ref, s32[1]{0:T(128)} %collective-permute-done.other_ref.far_ref.own_ref, s32[48]{0:T(128)S(1)} %collective-permute-done.3.far_cols, ...), custom_call_target="tpu_custom_call" | custom-call | flops 80000000000 | bytes 32000000 | tf_op jit(solution)/shard_map/weights/pallas_call | solution.py:206
  53.2 0.5 inner.3.refs_0_
  53.8 0.0 collective-permute-done.7.refs_0_
  53.8 1.7 %inner.4.refs_1_ = f32[4,8,128]{2,1,0:T(8,128)S(1)} custom-call(bf16[2,6,2,128,128]{4,3,2,1,0:T(8,128)(2,1)} %collective-permute-done.7.refs_0_, f32[4,6,2,2,128,128]{5,4,3,2,1,0:T(8,128)S(1)} %weights.2.refs_1_.refs_4_, f32[4,6,2,2,128,128]{5,4,3,2,1,0:T(8,128)S(1)} %weights.3.refs_2_.refs_5_), custom_call_target="tpu_custom_call" | custom-call | flops 4000000 | bytes 4000000 | tf_op jit(solution)/shard_map/inner/pallas_call | solution.py:257
  55.5 4.1 %collective-permute-done.8.refs_0_ = bf16[2,6,2,128,128]{4,3,2,1,0:T(8,128)(2,1)S(1)} collective-permute-done((bf16[2,6,2,128,128]{4,3,2,1,0:T(8,128)(2,1)S(1)}, bf16[2,6,2,128,128]{4,3,2,1,0:T(8,128)(2,1)S(1)}, u32[]{:S(2)}, u32[]{:S(2)}) %collective-permute-start.8) | collective-permute-done | bytes 786464 | tf_op jit(solution)/shard_map/ppermute | solution.py:313
  59.6 0.5 inner.5.refs_2_
  60.2 15.3 %collective-permute-done.9.refs_3_ = bf16[2,6,2,128,128]{4,3,2,1,0:T(8,128)(2,1)S(1)} collective-permute-done((bf16[2,6,2,128,128]{4,3,2,1,0:T(8,128)(2,1)S(1)}, bf16[2,6,2,128,128]{4,3,2,1,0:T(8,128)(2,1)S(1)}, u32[]{:S(2)}, u32[]{:S(2)}) %collective-permute-start.9) | collective-permute-done | bytes 786464 | tf_op jit(solution)/shard_map/ppermute | solution.py:313
  75.5 0.0 copy-done.6
  75.5 1.1 %last.1 = (f32[2,2,1]{2,1,0:T(2,128)S(1)}, f32[2,2,1]{2,1,0:T(2,128)S(1)}) custom-call(s32[1]{0:T(128)} %bitcast.core_ref, s32[4]{0:T(128)S(1)} %copy-done.5, s32[8]{0:T(128)S(1)} %copy-done.6, f32[4,8,128]{2,1,0:T(8,128)S(1)} %inner.3.refs_0_, f32[4,8,128]{2,1,0:T(8,128)S(1)} %inner.4.refs_1_, f32[4,8,128]{2,1,0:T(8,128)S(1)} %inner.5.refs_2_, ...), custom_call_target="tpu_custom_call" | custom-call | flops 4000000 | bytes 4000000 | tf_op jit(solution)/shard_map/last/pallas_call | solution.py:294
  76.6 1.3 %collective-permute-start.12 = (f32[2,2,1]{2,1,0:T(2,128)S(1)}, f32[2,2,1]{2,1,0:T(2,128)S(1)}, u32[]{:S(2)}, u32[]{:S(2)}) collective-permute-start(f32[2,2,1]{2,1,0:T(2,128)S(1)} %get-tuple-element.18), channel_id=1, source_target_pairs={{0,9},{1,8},{2,11},{3,10},{12,5},{13,4},{14,7},{15,6},{16,25},{17,... | collective-permute-start | bytes 56 | tf_op jit(solution)/shard_map/ppermute | solution.py:338
  77.9 0.1 collective-permute-start.10
  78.0 1.3 %collective-permute-start.11 = (f32[2,2,1]{2,1,0:T(2,128)S(1)}, f32[2,2,1]{2,1,0:T(2,128)S(1)}, u32[]{:S(2)}, u32[]{:S(2)}) collective-permute-start(f32[2,2,1]{2,1,0:T(2,128)S(1)} %get-tuple-element.17), channel_id=1, source_target_pairs={{0,8},{1,9},{2,10},{3,11},{12,4},{13,5},{14,6},{15,7},{16,24},{17,... | collective-permute-start | bytes 56 | tf_op jit(solution)/shard_map/ppermute | solution.py:338
  79.3 3.1 %collective-permute-done.12 = f32[2,2,1]{2,1,0:T(2,128)S(1)} collective-permute-done((f32[2,2,1]{2,1,0:T(2,128)S(1)}, f32[2,2,1]{2,1,0:T(2,128)S(1)}, u32[]{:S(2)}, u32[]{:S(2)}) %collective-permute-start.12) | collective-permute-done | bytes 48 | tf_op jit(solution)/shard_map/ppermute | solution.py:338
  82.4 2.0 %collective-permute-done.11 = f32[2,2,1]{2,1,0:T(2,128)S(1)} collective-permute-done((f32[2,2,1]{2,1,0:T(2,128)S(1)}, f32[2,2,1]{2,1,0:T(2,128)S(1)}, u32[]{:S(2)}, u32[]{:S(2)}) %collective-permute-start.11) | collective-permute-done | bytes 48 | tf_op jit(solution)/shard_map/ppermute | solution.py:338
  84.5 0.0 collective-permute-done.10
  84.5 0.7 copy.8
  (5 shorter events, 0.0 us)
Async XLA Ops:
  2.7 22.8 %collective-permute-start.1 = (bf16[2,6,2,128,128]{4,3,2,1,0:T(8,128)(2,1)}, bf16[2,6,2,128,128]{4,3,2,1,0:T(8,128)(2,1)S(1)}, u32[]{:S(2)}, u32[]{:S(2)}) collective-permute-start(bf16[2,6,2,128,128]{4,3,2,1,0:T(8,128)(2,1)} %pick_source.1.d_ref), channel_id=1, source_target_pairs={{8,0},{10,2},{4,12},{6,14},{9,1},{11,3},{5,13},{7,15},{24,16},{26,... | collective-permute-start | bytes 2359304 | tf_op jit(solution)/shard_map/ppermute | solution.py:313
  7.2 2.9 %collective-permute-start = (s32[1]{0:T(128)}, s32[1]{0:T(128)}, u32[]{:S(2)}, u32[]{:S(2)}) collective-permute-start(s32[1]{0:T(128)} %param.7), channel_id=1, source_target_pairs={{0,1},{1,0},{2,3},{3,2},{4,5},{5,4},{6,7},{7,6},{8,9},{9,8},{10,11... | collective-permute-start | bytes 20 | tf_op jit(solution)/shard_map/ppermute | solution.py:312
  8.2 17.2 %collective-permute-start.2 = (s32[48]{0:T(128)S(1)}, s32[48]{0:T(128)S(1)}, u32[]{:S(2)}, u32[]{:S(2)}) collective-permute-start(s32[48]{0:T(128)S(1)} %reshape.7.own_cols.b_cols), channel_id=1, source_target_pairs={{8,0},{10,2},{4,12},{6,14},{9,1},{11,3},{5,13},{7,15},{24,16},{26,... | collective-permute-start | bytes 584 | tf_op jit(solution)/shard_map/ppermute | solution.py:313
  9.5 26.9 %collective-permute-start.4 = (s32[48]{0:T(128)S(1)}, s32[48]{0:T(128)S(1)}, u32[]{:S(2)}, u32[]{:S(2)}) collective-permute-start(s32[48]{0:T(128)S(1)} %reshape.7.own_cols.b_cols), channel_id=1, source_target_pairs={{0,1},{1,0},{2,3},{3,2},{4,5},{5,4},{6,7},{7,6},{8,9},{9,8},{10,11... | collective-permute-start | bytes 584 | tf_op jit(solution)/shard_map/ppermute | solution.py:312
  10.1 33.0 %collective-permute-start.6 = (bf16[2,6,2,128,128]{4,3,2,1,0:T(8,128)(2,1)}, bf16[2,6,2,128,128]{4,3,2,1,0:T(8,128)(2,1)S(1)}, u32[]{:S(2)}, u32[]{:S(2)}) collective-permute-start(bf16[2,6,2,128,128]{4,3,2,1,0:T(8,128)(2,1)} %pick_source.1.d_ref), channel_id=1, source_target_pairs={{0,1},{1,0},{2,3},{3,2},{4,5},{5,4},{6,7},{7,6},{8,9},{9,8},{10,11... | collective-permute-start | bytes 2359304 | tf_op jit(solution)/shard_map/ppermute | solution.py:312
  12.1 1.9 %copy-start = (bf16[1,4,2,6,2,128,128]{6,5,4,3,2,1,0:T(8,128)(2,1)S(1)}, bf16[1,4,2,6,2,128,128]{6,5,4,3,2,1,0:T(8,128)(2,1)}, u32[]{:S(2)}) copy-start(bf16[1,4,2,6,2,128,128]{6,5,4,3,2,1,0:T(8,128)(2,1)} %param.5) | copy-start | bytes 9437188
  14.0 0.6 copy-start.3
  16.2 26.9 %copy-start.5 = (s32[4]{0:T(128)S(1)}, s32[4]{0:T(128)}, u32[]{:S(2)}) copy-start(s32[4]{0:T(128)} %get-tuple-element.12.order_ref) | copy-start | bytes 52
  16.2 26.9 %copy-start.1 = (bf16[1,4,2,6,2,128,128]{6,5,4,3,2,1,0:T(8,128)(2,1)S(1)}, bf16[1,4,2,6,2,128,128]{6,5,4,3,2,1,0:T(8,128)(2,1)}, u32[]{:S(2)}) copy-start(bf16[1,4,2,6,2,128,128]{6,5,4,3,2,1,0:T(8,128)(2,1)} %param.5) | copy-start | bytes 9437188
  16.3 37.5 %collective-permute-start.7 = (bf16[2,6,2,128,128]{4,3,2,1,0:T(8,128)(2,1)}, bf16[2,6,2,128,128]{4,3,2,1,0:T(8,128)(2,1)}, u32[]{:S(2)}, u32[]{:S(2)}) collective-permute-start(bf16[2,6,2,128,128]{4,3,2,1,0:T(8,128)(2,1)} %get-tuple-element.14), channel_id=1, source_target_pairs={{8,0},{10,2},{4,12},{6,14},{9,1},{11,3},{5,13},{7,15},{24,16},{26,... | collective-permute-start | bytes 2359304 | tf_op jit(solution)/shard_map/ppermute | solution.py:313
  25.4 16.3 %collective-permute-start.3 = (s32[48]{0:T(128)S(1)}, s32[48]{0:T(128)S(1)}, u32[]{:S(2)}, u32[]{:S(2)}) collective-permute-start(s32[48]{0:T(128)S(1)} %collective-permute-done.2.far_cols.m_cols), channel_id=1, source_target_pairs={{0,1},{1,0},{2,3},{3,2},{4,5},{5,4},{6,7},{7,6},{8,9},{9,8},{10,11... | collective-permute-start | bytes 584 | tf_op jit(solution)/shard_map/ppermute | solution.py:312
  25.4 17.7 %collective-permute-start.5 = (bf16[2,6,2,128,128]{4,3,2,1,0:T(8,128)(2,1)S(1)}, bf16[2,6,2,128,128]{4,3,2,1,0:T(8,128)(2,1)S(1)}, u32[]{:S(2)}, u32[]{:S(2)}) collective-permute-start(bf16[2,6,2,128,128]{4,3,2,1,0:T(8,128)(2,1)S(1)} %collective-permute-done.1.a_ref.refs_0_), channel_id=1, source_target_pairs={{0,1},{1,0},{2,3},{3,2},{4,5},{5,4},{6,7},{7,6},{8,9},{9,8},{10,11... | collective-permute-start | bytes 2359304 | tf_op jit(solution)/shard_map/ppermute | solution.py:312
  26.0 1.1 %copy-start.2 = (bf16[2,6,2,128,128]{4,3,2,1,0:T(8,128)(2,1)S(1)}, bf16[2,6,2,128,128]{4,3,2,1,0:T(8,128)(2,1)}, u32[]{:S(2)}) copy-start(bf16[2,6,2,128,128]{4,3,2,1,0:T(8,128)(2,1)} %pick_source.1.d_ref) | copy-start | bytes 2359300
  27.1 0.6 copy-start.4
  36.4 23.2 %collective-permute-start.8 = (bf16[2,6,2,128,128]{4,3,2,1,0:T(8,128)(2,1)S(1)}, bf16[2,6,2,128,128]{4,3,2,1,0:T(8,128)(2,1)S(1)}, u32[]{:S(2)}, u32[]{:S(2)}) collective-permute-start(bf16[2,6,2,128,128]{4,3,2,1,0:T(8,128)(2,1)S(1)} %get-tuple-element.15), channel_id=1, source_target_pairs={{8,0},{10,2},{4,12},{6,14},{9,1},{11,3},{5,13},{7,15},{24,16},{26,... | collective-permute-start | bytes 2359304 | tf_op jit(solution)/shard_map/ppermute | solution.py:313
  41.8 33.7 %collective-permute-start.9 = (bf16[2,6,2,128,128]{4,3,2,1,0:T(8,128)(2,1)S(1)}, bf16[2,6,2,128,128]{4,3,2,1,0:T(8,128)(2,1)S(1)}, u32[]{:S(2)}, u32[]{:S(2)}) collective-permute-start(bf16[2,6,2,128,128]{4,3,2,1,0:T(8,128)(2,1)S(1)} %get-tuple-element.16), channel_id=1, source_target_pairs={{8,0},{10,2},{4,12},{6,14},{9,1},{11,3},{5,13},{7,15},{24,16},{26,... | collective-permute-start | bytes 2359304 | tf_op jit(solution)/shard_map/ppermute | solution.py:313
  55.5 20.0 %copy-start.6 = (s32[8]{0:T(128)S(1)}, s32[8]{0:T(128)}, u32[]{:S(2)}) copy-start(s32[8]{0:T(128)} %get-tuple-element.13.sinks_ref) | copy-start | bytes 100
  76.6 5.8 %collective-permute-start.12 = (f32[2,2,1]{2,1,0:T(2,128)S(1)}, f32[2,2,1]{2,1,0:T(2,128)S(1)}, u32[]{:S(2)}, u32[]{:S(2)}) collective-permute-start(f32[2,2,1]{2,1,0:T(2,128)S(1)} %get-tuple-element.18), channel_id=1, source_target_pairs={{0,9},{1,8},{2,11},{3,10},{12,5},{13,4},{14,7},{15,6},{16,25},{17,... | collective-permute-start | bytes 56 | tf_op jit(solution)/shard_map/ppermute | solution.py:338
  77.9 6.5 %collective-permute-start.10 = (f32[2,2,1]{2,1,0:T(2,128)S(1)}, f32[2,2,1]{2,1,0:T(2,128)S(1)}, u32[]{:S(2)}, u32[]{:S(2)}) collective-permute-start(f32[2,2,1]{2,1,0:T(2,128)S(1)} %get-tuple-element.18), channel_id=1, source_target_pairs={{0,1},{1,0},{2,3},{3,2},{4,5},{5,4},{6,7},{7,6},{8,9},{9,8},{10,11... | collective-permute-start | bytes 56 | tf_op jit(solution)/shard_map/ppermute | solution.py:312
  78.0 6.5 %collective-permute-start.11 = (f32[2,2,1]{2,1,0:T(2,128)S(1)}, f32[2,2,1]{2,1,0:T(2,128)S(1)}, u32[]{:S(2)}, u32[]{:S(2)}) collective-permute-start(f32[2,2,1]{2,1,0:T(2,128)S(1)} %get-tuple-element.17), channel_id=1, source_target_pairs={{0,8},{1,9},{2,10},{3,11},{12,4},{13,5},{14,6},{15,7},{16,24},{17,... | collective-permute-start | bytes 56 | tf_op jit(solution)/shard_map/ppermute | solution.py:338

commit v4 on v3

--- a/solution.py
+++ b/solution.py
@@ -69,7 +69,7 @@
     )(order, fields)
 
 
-def plan_kernel(core_ref, own_ref, other_ref, deltas_ref, order_ref, sinks_ref):
+def plan_kernel(core_ref, own_ref, other_ref, deltas_ref, order_ref, sinks_ref, full_ref):
     times = order_ref.shape[0]
     deltas = deltas_ref.shape[0]
     sinks = []
@@ -93,6 +93,16 @@
             if other != t:
                 rank += (keys[other] < keys[t]).astype(I32)
         order_ref[rank] = I32(t)
+    full = I32(0)
+    for c in range(2):
+        count = I32(0)
+        for t in range(times):
+            needed = (own_ref[0] == c * times + t) | (other_ref[0] == c * times + t)
+            for sink in sinks:
+                needed = needed | (sink == c * times + t)
+            count += needed.astype(I32)
+        full += jnp.where(count == times, I32(1 << c), I32(0))
+    full_ref[0] = full
 
 
 def plan(core, own, other, deltas, times):
@@ -101,9 +111,10 @@
         out_shape=[
             jax.ShapeDtypeStruct((times,), I32),
             jax.ShapeDtypeStruct((2 * deltas.shape[0],), I32),
+            jax.ShapeDtypeStruct((1,), I32),
         ],
         in_specs=[SMEM] * 4,
-        out_specs=[SMEM] * 2,
+        out_specs=[SMEM] * 3,
         cost_estimate=cost(0, 1000),
         name="plan",
     )(core, own, other, deltas)
@@ -199,7 +210,7 @@
                 u_ref[0, r, k, 1] -= part[size:, k * size : (k + 1) * size]
 
 
-def weights(order, far_time, own_time, far_cols, own_cols, m_cols, b_cols, a, d, fields):
+def weights(flops, order, far_time, own_time, far_cols, own_cols, m_cols, b_cols, a, d, fields):
     times = fields.shape[0]
     _, rows, per_row, size, _ = a.shape
     whole = lambda slot, *_: (0, 0, 0, 0, 0)
@@ -225,7 +236,7 @@
             ],
         ),
         compiler_params=pltpu.CompilerParams(vmem_limit_bytes=24 * 2**20),
-        cost_estimate=cost(times * 20_000_000_000, times * 8_000_000),
+        cost_estimate=cost(flops, times * 1_000_000),
         name="weights",
     )(order, far_time, own_time, far_cols, own_cols, m_cols, b_cols, a, d, fields)
 
@@ -266,13 +277,13 @@
 
 
 def last_kernel(core_ref, order_ref, sinks_ref, *refs):
-    *earlier, field_ref, u0_ref, u1_ref, mine_ref, theirs_ref = refs
+    *others, field_ref, u0_ref, u1_ref, mine_ref, theirs_ref = refs
     slots = order_ref.shape[0]
     deltas = sinks_ref.shape[0] // 2
     share = deltas // 2
     core = core_ref[0]
-    sums = [[ref[at] for at in range(4)] for ref in earlier]
-    sums.append(products(field_ref, (u0_ref, u1_ref), slots - 1))
+    sums = [[ref[at] for at in range(4)] for ref in others]
+    sums.insert(slots - 2, products(field_ref, (u0_ref, u1_ref), slots - 2))
     for out_ref, owner in ((mine_ref, core), (theirs_ref, 1 - core)):
         lines = [jnp.zeros(sums[0][0].shape, F32) for _ in range(2 * share)]
         for slot in range(slots):
@@ -289,17 +300,17 @@
             out_ref[part] = table[part * share : (part + 1) * share]
 
 
-def last(core, order, sinks, earlier, field, u0, u1):
+def last(core, order, sinks, others, field, u0, u1):
     share = sinks.shape[0] // 4
     return pl.pallas_call(
         last_kernel,
         out_shape=[jax.ShapeDtypeStruct((2, share, 1), F32)] * 2,
-        in_specs=[SMEM] * 3 + [VMEM] * (len(earlier) + 3),
+        in_specs=[SMEM] * 3 + [VMEM] * (len(others) + 3),
         out_specs=[VMEM] * 2,
         cost_estimate=cost(4_000_000, 4_000_000),
         compiler_params=pltpu.CompilerParams(vmem_limit_bytes=24 * 2**20),
         name="last",
-    )(core, order, sinks, *earlier, field, u0, u1)
+    )(core, order, sinks, *others, field, u0, u1)
 
 
 def local(fields, block_cols, sources, deltas, partner):
@@ -318,21 +329,45 @@
     far = [to_partner(own_field)]
 
     other_time = swap(sources)
-    order, sinks = plan(core, sources, other_time, deltas, times)
-    far += [to_partner(field) for field in pick_others(order, fields)]
+    order, sinks, full = plan(core, sources, other_time, deltas, times)
+    *early, late = pick_others(order, fields)
+    for field in early:
+        if len(far) > 1:
+            field, far[-2] = lax.optimization_barrier((field, far[-2]))
+        far.append(to_partner(field))
 
     other_cols = swap(cols)
     far_other_cols = swap(far_cols)
     other_field = swap(own_field)
     far_other = swap(far[0])
-    u0 = weights(order, sources, sources, far_cols, cols, far_cols, cols, far[0], own_field, fields)
+    u0 = weights(80_000_000_000, order, sources, sources, far_cols, cols, far_cols, cols, far[0], own_field, fields)
     u1 = weights(
-        order, other_time, other_time, far_other_cols, other_cols, far_cols, cols, far_other, other_field, fields
+        2_000_000_000,
+        order,
+        other_time,
+        other_time,
+        far_other_cols,
+        other_cols,
+        far_cols,
+        cols,
+        far_other,
+        other_field,
+        fields,
     )
-    earlier = [inner(slot, far[slot], u0, u1) for slot in range(times - 1)]
-    mine, theirs = last(core, order, sinks, earlier, far[-1], u0, u1)
+    sums = [inner(slot, far[slot], u0, u1) for slot in range(times - 2)]
 
     both = ("mom", "src")
+
+    def last_slot(cores):
+        routes = [(2 * a + c, 2 * b + c) for a, b in pairs for c in cores]
+        return lambda field, u0, u1: inner(times - 1, lax.ppermute(field, both, routes), u0, u1)
+
+    no_slot = lambda field, u0, u1: jnp.zeros(sums[0].shape, F32)
+    branches = [no_slot, last_slot([0]), last_slot([1]), last_slot([0, 1])]
+    late, *sums = lax.optimization_barrier((late, *sums))
+    sums.append(lax.switch(full[0], branches, late, u0, u1))
+    mine, theirs = last(core, order, sinks, sums, far[-1], u0, u1)
+
     straight = [(2 * a + c, 2 * b + c) for b, a in pairs for c in range(2)]
     crossed = [(2 * a + c, 2 * b + 1 - c) for b, a in pairs for c in range(2)]
     return mine + swap(theirs) + lax.ppermute(mine, both, straight) + lax.ppermute(theirs, both, crossed)

time: 85.6 us -> 81.2 us (0.949)
  waiting for transfers between devices: 31.3 us -> 14.9 us
  starting transfers between devices: 18.9 us -> 25.3 us
  Pallas kernels: 28.3 us -> 32.1 us
  local copies, waits for them, and re-layouts: 5.79 us -> 7 us
    ppermute x5 -> x4, waiting for transfers between devices: 26.1 us -> 9.77 us  [local(): to_partner = lambda value: lax.ppermute(value, 'mom', pairs)]
    ppermute x6, starting transfers between devices: 1.29 us -> 9.34 us  [local(): swap = lambda value: lax.ppermute(value, 'src', [(0, 1), (1, 0)])]
    pallas_call x1, Pallas kernels: 1.13 us -> 5.18 us  [last(): pl.pallas_call(last_kernel, out_shape=[jax.ShapeDtypeStruct((2, share, 1)...]
    ppermute x1, waiting for transfers between devices: 3.12 us -> 0.01 us  [local(): lax.ppermute(theirs, both, crossed)]
    ppermute x1, waiting for transfers between devices: 2.04 us -> 5.08 us  [local(): lax.ppermute(mine, both, straight)]
    ppermute x5 -> x4, starting transfers between devices: 15 us -> 12.7 us  [local(): to_partner = lambda value: lax.ppermute(value, 'mom', pairs)]
    unnamed x15 -> x21, local copies, waits for them, and re-layouts: 5.04 us -> 6.25 us
  transfers between devices with their start and end apart: 13 -> 13, of which waited for: 5 -> 3; matrix products, arithmetic and copies ran while one was open for 1% -> 1% of each run, Pallas kernels for 30% -> 31%
where the time goes in v4:
time: 81.2 us; the launch traced here: 80.8 us
  Pallas kernels  32.1 us (40%)
  starting transfers between devices  25.3 us (31%)
  waiting for transfers between devices  14.9 us (18%)
  local copies, waits for them, and re-layouts  7 us (9%)
  between operations  1.48 us (2%)
    pallas_call x2, Pallas kernels, weights(): pl.pallas_call(weights_kernel, out_shape=jax.ShapeDtypeStruct((times, row...  19.1 us
    ppermute x4, starting transfers between devices, local(): to_partner = lambda value: lax.ppermute(value, 'mom', pairs)  12.7 us
    ppermute x4, waiting for transfers between devices, local(): to_partner = lambda value: lax.ppermute(value, 'mom', pairs)  9.77 us
    ppermute x6, starting transfers between devices, local(): swap = lambda value: lax.ppermute(value, 'src', [(0, 1), (1, 0)])  9.34 us
    unnamed x21, local copies, waits for them, and re-layouts  6.25 us
    pallas_call x1, Pallas kernels, last(): pl.pallas_call(last_kernel, out_shape=[jax.ShapeDtypeStruct((2, share, 1)...  5.18 us
    ppermute x1, waiting for transfers between devices, local(): lax.ppermute(mine, both, straight)  5.08 us
    pallas_call x3, Pallas kernels, inner(): pl.pallas_call(lambda *refs: inner_kernel(slot, *refs), out_shape=jax.Sha...  2.06 us
  transfers between devices with their start and end apart: 13, of which 3 were waited for; matrix products, arithmetic and copies ran while one was open for 1% of the time, Pallas kernels for 31%

profile of v4, /device:TPU:8, one launch (start us, length us, event | category | flops | bytes accessed | tf_op | source)
XLA Modules:
  0.0 80.8 jit_solution(11729638135813561045)
XLA Ops:
  0.7 2.0 %pick_source.1.d_ref = bf16[2,6,2,128,128]{4,3,2,1,0:T(8,128)(2,1)} custom-call(s32[1]{0:T(128)S(6)} %copy.13.own_ref.source_ref.far_ref, bf16[4,2,6,2,128,128]{5,4,3,2,1,0:T(8,128)(2,1)} %bitcast.3), custom_call_target="tpu_custom_call" | custom-call | bytes 1600000 | tf_op jit(solution)/shard_map/pick_source/pallas_call | solution.py:34
  2.7 4.5 %collective-permute-start.4 = (bf16[2,6,2,128,128]{4,3,2,1,0:T(8,128)(2,1)}, bf16[2,6,2,128,128]{4,3,2,1,0:T(8,128)(2,1)S(1)}, u32[]{:S(2)}, u32[]{:S(2)}) collective-permute-start(bf16[2,6,2,128,128]{4,3,2,1,0:T(8,128)(2,1)} %pick_source.1.d_ref), channel_id=1, source_target_pairs={{8,0},{10,2},{4,12},{6,14},{9,1},{11,3},{5,13},{7,15},{24,16},{26,... | collective-permute-start | bytes 2359304 | tf_op jit(solution)/shard_map/ppermute | solution.py:324
  7.3 0.1 collective-permute-start.3
  7.3 0.8 copy.7
  8.1 0.1 reshape.10.own_cols.b_cols
  8.2 0.6 collective-permute-start.7
  8.8 1.3 %collective-permute-start.5 = (s32[48]{0:T(128)S(1)}, s32[48]{0:T(128)S(1)}, u32[]{:S(2)}, u32[]{:S(2)}) collective-permute-start(s32[48]{0:T(128)S(1)} %reshape.10.own_cols.b_cols), channel_id=1, source_target_pairs={{8,0},{10,2},{4,12},{6,14},{9,1},{11,3},{5,13},{7,15},{24,16},{26,... | collective-permute-start | bytes 584 | tf_op jit(solution)/shard_map/ppermute | solution.py:324
  10.1 0.1 collective-permute-start.9
  10.2 0.0 collective-permute-done.3.other_ref.far_ref.own_ref
  10.2 2.0 %plan.1 = (s32[4]{0:T(128)}, s32[8]{0:T(128)}, s32[1]{0:T(128)}) custom-call(s32[1]{0:T(128)} %bitcast.core_ref, s32[1]{0:T(128)S(6)} %copy.13.own_ref.source_ref.far_ref, s32[1]{0:T(128)} %collective-permute-done.3.other_ref.far_ref.own_ref, s32[4]{0:T(128)} %deltas_ref.1), custom_call_target="tpu_custom_call" | custom-call | bytes 1000 | tf_op jit(solution)/shard_map/plan/pallas_call | solution.py:109
  12.1 0.0 copy-start
  12.1 1.9 %copy-done = bf16[1,4,2,6,2,128,128]{6,5,4,3,2,1,0:T(8,128)(2,1)S(1)} copy-done((bf16[1,4,2,6,2,128,128]{6,5,4,3,2,1,0:T(8,128)(2,1)S(1)}, bf16[1,4,2,6,2,128,128]{6,5,4,3,2,1,0:T(8,128)(2,1)}, u32[]{:S(2)}) %copy-start) | copy-done | bytes 3145752
  14.0 0.6 copy-done.3
  14.6 1.7 %pick_others.1 = (bf16[2,6,2,128,128]{4,3,2,1,0:T(8,128)(2,1)S(1)}, bf16[2,6,2,128,128]{4,3,2,1,0:T(8,128)(2,1)S(1)}, bf16[2,6,2,128,128]{4,3,2,1,0:T(8,128)(2,1)}) custom-call(s32[4]{0:T(128)S(1)} %copy-done.3, bf16[4,2,6,2,128,128]{5,4,3,2,1,0:T(8,128)(2,1)S(1)} %bitcast.4), custom_call_target="tpu_custom_call" | custom-call | bytes 4800000 | tf_op jit(solution)/shard_map/pick_others/pallas_call | solution.py:60
  16.3 1.3 %collective-permute-start.10 = (bf16[2,6,2,128,128]{4,3,2,1,0:T(8,128)(2,1)S(1)}, bf16[2,6,2,128,128]{4,3,2,1,0:T(8,128)(2,1)S(1)}, u32[]{:S(2)}, u32[]{:S(2)}) collective-permute-start(bf16[2,6,2,128,128]{4,3,2,1,0:T(8,128)(2,1)S(1)} %get-tuple-element.55), channel_id=1, source_target_pairs={{8,0},{10,2},{4,12},{6,14},{9,1},{11,3},{5,13},{7,15},{24,16},{26,... | collective-permute-start | bytes 2359304 | tf_op jit(solution)/shard_map/ppermute | solution.py:324
  18.3 7.2 %collective-permute-done.5.far_cols.m_cols = s32[48]{0:T(128)S(1)} collective-permute-done((s32[48]{0:T(128)S(1)}, s32[48]{0:T(128)S(1)}, u32[]{:S(2)}, u32[]{:S(2)}) %collective-permute-start.5) | collective-permute-done | bytes 224 | tf_op jit(solution)/shard_map/ppermute | solution.py:324
  25.4 0.0 collective-permute-start.6
  25.5 0.0 collective-permute-done.4.a_ref.refs_0_
  25.5 5.6 %collective-permute-start.11 = (bf16[2,6,2,128,128]{4,3,2,1,0:T(8,128)(2,1)S(1)}, bf16[2,6,2,128,128]{4,3,2,1,0:T(8,128)(2,1)S(1)}, u32[]{:S(2)}, u32[]{:S(2)}) collective-permute-start(bf16[2,6,2,128,128]{4,3,2,1,0:T(8,128)(2,1)S(1)} %get-tuple-element.60), channel_id=1, source_target_pairs={{8,0},{10,2},{4,12},{6,14},{9,1},{11,3},{5,13},{7,15},{24,16},{26,... | collective-permute-start | bytes 2359304 | tf_op jit(solution)/shard_map/ppermute | solution.py:324
  31.0 0.0 collective-permute-done.7.own_cols
  31.0 0.3 collective-permute-start.8
  31.3 1.1 %copy-done.2 = bf16[2,6,2,128,128]{4,3,2,1,0:T(8,128)(2,1)S(1)} copy-done((bf16[2,6,2,128,128]{4,3,2,1,0:T(8,128)(2,1)S(1)}, bf16[2,6,2,128,128]{4,3,2,1,0:T(8,128)(2,1)}, u32[]{:S(2)}) %copy-start.2) | copy-done | bytes 786456
  32.5 0.6 copy-done.4
  33.1 9.0 %weights.2.refs_1_.refs_4_ = f32[4,6,2,2,128,128]{5,4,3,2,1,0:T(8,128)S(1)} custom-call(s32[4]{0:T(128)S(1)} %copy-done.4, s32[1]{0:T(128)S(6)} %copy.13.own_ref.source_ref.far_ref, s32[1]{0:T(128)S(6)} %copy.13.own_ref.source_ref.far_ref, s32[48]{0:T(128)S(1)} %collective-permute-done.5.far_cols.m_cols, s32[48]{0:T(128)S(1)} %reshape.10.own_cols.b_cols, ...), custom_call_target="tpu_custom_call" | custom-call | flops 80000000000 | bytes 4000000 | tf_op jit(solution)/shard_map/weights/pallas_call | solution.py:217
  42.1 0.0 copy-start.8
  42.1 0.0 collective-permute-done.6.far_cols
  42.1 0.0 collective-permute-done.9.d_ref
  42.1 0.0 collective-permute-done.8.a_ref
  42.1 0.0 copy-done.1
  42.1 10.1 %weights.3.refs_2_.refs_5_ = f32[4,6,2,2,128,128]{5,4,3,2,1,0:T(8,128)S(1)} custom-call(s32[4]{0:T(128)S(1)} %copy-done.4, s32[1]{0:T(128)} %collective-permute-done.3.other_ref.far_ref.own_ref, s32[1]{0:T(128)} %collective-permute-done.3.other_ref.far_ref.own_ref, s32[48]{0:T(128)S(1)} %collective-permute-done.6.far_cols, ...), custom_call_target="tpu_custom_call" | custom-call | flops 2000000000 | bytes 4000000 | tf_op jit(solution)/shard_map/weights/pallas_call | solution.py:217
  52.3 0.7 inner.8.refs_0_
  53.0 0.0 collective-permute-done.10.refs_0_
  53.0 0.7 inner.9.refs_1_
  53.7 1.0 %copy-done.9 = bf16[2,6,2,128,128]{4,3,2,1,0:T(8,128)(2,1)S(1)} copy-done((bf16[2,6,2,128,128]{4,3,2,1,0:T(8,128)(2,1)S(1)}, bf16[2,6,2,128,128]{4,3,2,1,0:T(8,128)(2,1)}, u32[]{:S(2)}) %copy-start.9) | copy-done | bytes 786456
  54.7 0.2 copy-done.7
  54.9 1.4 %conditional.1 = (f32[4,8,128]{2,1,0:T(8,128)S(1)}) conditional(s32[]{:T(128)} %bitcast.2, () %tuple.21, (bf16[2,6,2,128,128]{4,3,2,1,0:T(8,128)(2,1)S(1)}, f32[4,6,2,2,128,128]{5,4,3,2,1,0:T(8,128)S(1)}, f32[4,6,2,2,128,128]{5,4,3,2,1,0:T(8,128)S(1)}) %tuple.27, (bf16[2,6,2,128,128]{4,3,2,1,0:T(8,128)(2,1)S(1)}, ...), branch_computations={%region_0.0_spmd, %region_1.0_spmd, %region_2.0_spmd, %region_3.0_... | conditional | flops 4000000 | bytes 7145776 | solution.py:368
  54.9 0.7 collective-permute-start.1
  55.6 0.0 collective-permute-done.1.refs_0_
  55.6 0.7 inner.6
  56.3 2.6 %collective-permute-done.11.refs_3_ = bf16[2,6,2,128,128]{4,3,2,1,0:T(8,128)(2,1)S(1)} collective-permute-done((bf16[2,6,2,128,128]{4,3,2,1,0:T(8,128)(2,1)S(1)}, bf16[2,6,2,128,128]{4,3,2,1,0:T(8,128)(2,1)S(1)}, u32[]{:S(2)}, u32[]{:S(2)}) %collective-permute-start.11) | collective-permute-done | bytes 786464 | tf_op jit(solution)/shard_map/ppermute | solution.py:324
  58.9 5.2 %last.1 = (f32[2,2,1]{2,1,0:T(2,128)S(1)}, f32[2,2,1]{2,1,0:T(2,128)S(1)}) custom-call(s32[1]{0:T(128)} %bitcast.core_ref, s32[4]{0:T(128)S(1)} %copy-done.5, s32[8]{0:T(128)S(1)} %copy-done.6, f32[4,8,128]{2,1,0:T(8,128)S(1)} %inner.8.refs_0_, f32[4,8,128]{2,1,0:T(8,128)S(1)} %inner.9.refs_1_, f32[4,8,128]{2,1,0:T(8,128)S(1)} %get-tuple-element.63.refs_2_, ...), custom_call_target="tpu_custom_call" | custom-call | flops 4000000 | bytes 4000000 | tf_op jit(solution)/shard_map/last/pallas_call | solution.py:305
  64.1 1.3 %collective-permute-start.14 = (f32[2,2,1]{2,1,0:T(2,128)S(1)}, f32[2,2,1]{2,1,0:T(2,128)S(1)}, u32[]{:S(2)}, u32[]{:S(2)}) collective-permute-start(f32[2,2,1]{2,1,0:T(2,128)S(1)} %get-tuple-element.62), channel_id=1, source_target_pairs={{0,9},{1,8},{2,11},{3,10},{12,5},{13,4},{14,7},{15,6},{16,25},{17,... | collective-permute-start | bytes 56 | tf_op jit(solution)/shard_map/ppermute | solution.py:373
  65.4 8.3 %collective-permute-start.12 = (f32[2,2,1]{2,1,0:T(2,128)S(1)}, f32[2,2,1]{2,1,0:T(2,128)S(1)}, u32[]{:S(2)}, u32[]{:S(2)}) collective-permute-start(f32[2,2,1]{2,1,0:T(2,128)S(1)} %get-tuple-element.62), channel_id=1, source_target_pairs={{0,1},{1,0},{2,3},{3,2},{4,5},{5,4},{6,7},{7,6},{8,9},{9,8},{10,11... | collective-permute-start | bytes 56 | tf_op jit(solution)/shard_map/ppermute | solution.py:323
  73.7 1.3 %collective-permute-start.13 = (f32[2,2,1]{2,1,0:T(2,128)S(1)}, f32[2,2,1]{2,1,0:T(2,128)S(1)}, u32[]{:S(2)}, u32[]{:S(2)}) collective-permute-start(f32[2,2,1]{2,1,0:T(2,128)S(1)} %get-tuple-element.61), channel_id=1, source_target_pairs={{0,8},{1,9},{2,10},{3,11},{12,4},{13,5},{14,6},{15,7},{16,24},{17,... | collective-permute-start | bytes 56 | tf_op jit(solution)/shard_map/ppermute | solution.py:373
  75.0 5.1 %collective-permute-done.13 = f32[2,2,1]{2,1,0:T(2,128)S(1)} collective-permute-done((f32[2,2,1]{2,1,0:T(2,128)S(1)}, f32[2,2,1]{2,1,0:T(2,128)S(1)}, u32[]{:S(2)}, u32[]{:S(2)}) %collective-permute-start.13) | collective-permute-done | bytes 48 | tf_op jit(solution)/shard_map/ppermute | solution.py:373
  80.1 0.0 collective-permute-done.14
  80.1 0.0 collective-permute-done.12
  80.1 0.7 copy.8
  (12 shorter events, 0.0 us)
Async XLA Ops:
  2.7 22.8 %collective-permute-start.4 = (bf16[2,6,2,128,128]{4,3,2,1,0:T(8,128)(2,1)}, bf16[2,6,2,128,128]{4,3,2,1,0:T(8,128)(2,1)S(1)}, u32[]{:S(2)}, u32[]{:S(2)}) collective-permute-start(bf16[2,6,2,128,128]{4,3,2,1,0:T(8,128)(2,1)} %pick_source.1.d_ref), channel_id=1, source_target_pairs={{8,0},{10,2},{4,12},{6,14},{9,1},{11,3},{5,13},{7,15},{24,16},{26,... | collective-permute-start | bytes 2359304 | tf_op jit(solution)/shard_map/ppermute | solution.py:324
  7.3 2.9 %collective-permute-start.3 = (s32[1]{0:T(128)}, s32[1]{0:T(128)}, u32[]{:S(2)}, u32[]{:S(2)}) collective-permute-start(s32[1]{0:T(128)} %param.11), channel_id=1, source_target_pairs={{0,1},{1,0},{2,3},{3,2},{4,5},{5,4},{6,7},{7,6},{8,9},{9,8},{10,11... | collective-permute-start | bytes 20 | tf_op jit(solution)/shard_map/ppermute | solution.py:323
  8.2 22.8 %collective-permute-start.7 = (s32[48]{0:T(128)S(1)}, s32[48]{0:T(128)S(1)}, u32[]{:S(2)}, u32[]{:S(2)}) collective-permute-start(s32[48]{0:T(128)S(1)} %reshape.10.own_cols.b_cols), channel_id=1, source_target_pairs={{0,1},{1,0},{2,3},{3,2},{4,5},{5,4},{6,7},{7,6},{8,9},{9,8},{10,11... | collective-permute-start | bytes 584 | tf_op jit(solution)/shard_map/ppermute | solution.py:323
  8.8 16.7 %collective-permute-start.5 = (s32[48]{0:T(128)S(1)}, s32[48]{0:T(128)S(1)}, u32[]{:S(2)}, u32[]{:S(2)}) collective-permute-start(s32[48]{0:T(128)S(1)} %reshape.10.own_cols.b_cols), channel_id=1, source_target_pairs={{8,0},{10,2},{4,12},{6,14},{9,1},{11,3},{5,13},{7,15},{24,16},{26,... | collective-permute-start | bytes 584 | tf_op jit(solution)/shard_map/ppermute | solution.py:324
  10.1 32.0 %collective-permute-start.9 = (bf16[2,6,2,128,128]{4,3,2,1,0:T(8,128)(2,1)}, bf16[2,6,2,128,128]{4,3,2,1,0:T(8,128)(2,1)S(1)}, u32[]{:S(2)}, u32[]{:S(2)}) collective-permute-start(bf16[2,6,2,128,128]{4,3,2,1,0:T(8,128)(2,1)} %pick_source.1.d_ref), channel_id=1, source_target_pairs={{0,1},{1,0},{2,3},{3,2},{4,5},{5,4},{6,7},{7,6},{8,9},{9,8},{10,11... | collective-permute-start | bytes 2359304 | tf_op jit(solution)/shard_map/ppermute | solution.py:323
  12.1 1.9 %copy-start = (bf16[1,4,2,6,2,128,128]{6,5,4,3,2,1,0:T(8,128)(2,1)S(1)}, bf16[1,4,2,6,2,128,128]{6,5,4,3,2,1,0:T(8,128)(2,1)}, u32[]{:S(2)}) copy-start(bf16[1,4,2,6,2,128,128]{6,5,4,3,2,1,0:T(8,128)(2,1)} %param.9) | copy-start | bytes 9437188
  14.0 0.6 copy-start.3
  16.3 36.7 %collective-permute-start.10 = (bf16[2,6,2,128,128]{4,3,2,1,0:T(8,128)(2,1)S(1)}, bf16[2,6,2,128,128]{4,3,2,1,0:T(8,128)(2,1)S(1)}, u32[]{:S(2)}, u32[]{:S(2)}) collective-permute-start(bf16[2,6,2,128,128]{4,3,2,1,0:T(8,128)(2,1)S(1)} %get-tuple-element.55), channel_id=1, source_target_pairs={{8,0},{10,2},{4,12},{6,14},{9,1},{11,3},{5,13},{7,15},{24,16},{26,... | collective-permute-start | bytes 2359304 | tf_op jit(solution)/shard_map/ppermute | solution.py:324
  25.4 16.7 %collective-permute-start.6 = (s32[48]{0:T(128)S(1)}, s32[48]{0:T(128)S(1)}, u32[]{:S(2)}, u32[]{:S(2)}) collective-permute-start(s32[48]{0:T(128)S(1)} %collective-permute-done.5.far_cols.m_cols), channel_id=1, source_target_pairs={{0,1},{1,0},{2,3},{3,2},{4,5},{5,4},{6,7},{7,6},{8,9},{9,8},{10,11... | collective-permute-start | bytes 584 | tf_op jit(solution)/shard_map/ppermute | solution.py:323
  25.5 16.7 %copy-start.1 = (bf16[1,4,2,6,2,128,128]{6,5,4,3,2,1,0:T(8,128)(2,1)S(1)}, bf16[1,4,2,6,2,128,128]{6,5,4,3,2,1,0:T(8,128)(2,1)}, u32[]{:S(2)}) copy-start(bf16[1,4,2,6,2,128,128]{6,5,4,3,2,1,0:T(8,128)(2,1)} %param.9) | copy-start | bytes 9437188
  25.5 33.4 %collective-permute-start.11 = (bf16[2,6,2,128,128]{4,3,2,1,0:T(8,128)(2,1)S(1)}, bf16[2,6,2,128,128]{4,3,2,1,0:T(8,128)(2,1)S(1)}, u32[]{:S(2)}, u32[]{:S(2)}) collective-permute-start(bf16[2,6,2,128,128]{4,3,2,1,0:T(8,128)(2,1)S(1)} %get-tuple-element.60), channel_id=1, source_target_pairs={{8,0},{10,2},{4,12},{6,14},{9,1},{11,3},{5,13},{7,15},{24,16},{26,... | collective-permute-start | bytes 2359304 | tf_op jit(solution)/shard_map/ppermute | solution.py:324
  31.0 11.1 %collective-permute-start.8 = (bf16[2,6,2,128,128]{4,3,2,1,0:T(8,128)(2,1)S(1)}, bf16[2,6,2,128,128]{4,3,2,1,0:T(8,128)(2,1)S(1)}, u32[]{:S(2)}, u32[]{:S(2)}) collective-permute-start(bf16[2,6,2,128,128]{4,3,2,1,0:T(8,128)(2,1)S(1)} %collective-permute-done.4.a_ref.refs_0_), channel_id=1, source_target_pairs={{0,1},{1,0},{2,3},{3,2},{4,5},{5,4},{6,7},{7,6},{8,9},{9,8},{10,11... | collective-permute-start | bytes 2359304 | tf_op jit(solution)/shard_map/ppermute | solution.py:323
  31.3 1.1 %copy-start.2 = (bf16[2,6,2,128,128]{4,3,2,1,0:T(8,128)(2,1)S(1)}, bf16[2,6,2,128,128]{4,3,2,1,0:T(8,128)(2,1)}, u32[]{:S(2)}) copy-start(bf16[2,6,2,128,128]{4,3,2,1,0:T(8,128)(2,1)} %pick_source.1.d_ref) | copy-start | bytes 2359300
  32.4 0.6 copy-start.4
  42.1 12.6 %copy-start.8 = (f32[4,6,2,2,128,128]{5,4,3,2,1,0:T(8,128)}, f32[4,6,2,2,128,128]{5,4,3,2,1,0:T(8,128)S(1)}, u32[]{:S(2)}) copy-start(f32[4,6,2,2,128,128]{5,4,3,2,1,0:T(8,128)S(1)} %weights.2.refs_1_.refs_4_) | copy-start | bytes 18874372
  52.3 2.6 %copy-start.7 = (f32[4,6,2,2,128,128]{5,4,3,2,1,0:T(8,128)}, f32[4,6,2,2,128,128]{5,4,3,2,1,0:T(8,128)S(1)}, u32[]{:S(2)}) copy-start(f32[4,6,2,2,128,128]{5,4,3,2,1,0:T(8,128)S(1)} %weights.3.refs_2_.refs_5_) | copy-start | bytes 18874372
  53.0 1.7 %copy-start.9 = (bf16[2,6,2,128,128]{4,3,2,1,0:T(8,128)(2,1)S(1)}, bf16[2,6,2,128,128]{4,3,2,1,0:T(8,128)(2,1)}, u32[]{:S(2)}) copy-start(bf16[2,6,2,128,128]{4,3,2,1,0:T(8,128)(2,1)} %get-tuple-element.59) | copy-start | bytes 2359300
  54.7 4.2 %copy-start.5 = (s32[4]{0:T(128)S(1)}, s32[4]{0:T(128)}, u32[]{:S(2)}) copy-start(s32[4]{0:T(128)} %get-tuple-element.50.order_ref) | copy-start | bytes 52
  54.7 4.2 %copy-start.6 = (s32[8]{0:T(128)S(1)}, s32[8]{0:T(128)}, u32[]{:S(2)}) copy-start(s32[8]{0:T(128)} %get-tuple-element.51.sinks_ref) | copy-start | bytes 100
  54.9 0.7 collective-permute-start.1
  64.1 16.0 %collective-permute-start.14 = (f32[2,2,1]{2,1,0:T(2,128)S(1)}, f32[2,2,1]{2,1,0:T(2,128)S(1)}, u32[]{:S(2)}, u32[]{:S(2)}) collective-permute-start(f32[2,2,1]{2,1,0:T(2,128)S(1)} %get-tuple-element.62), channel_id=1, source_target_pairs={{0,9},{1,8},{2,11},{3,10},{12,5},{13,4},{14,7},{15,6},{16,25},{17,... | collective-permute-start | bytes 56 | tf_op jit(solution)/shard_map/ppermute | solution.py:373
  65.4 14.7 %collective-permute-start.12 = (f32[2,2,1]{2,1,0:T(2,128)S(1)}, f32[2,2,1]{2,1,0:T(2,128)S(1)}, u32[]{:S(2)}, u32[]{:S(2)}) collective-permute-start(f32[2,2,1]{2,1,0:T(2,128)S(1)} %get-tuple-element.62), channel_id=1, source_target_pairs={{0,1},{1,0},{2,3},{3,2},{4,5},{5,4},{6,7},{7,6},{8,9},{9,8},{10,11... | collective-permute-start | bytes 56 | tf_op jit(solution)/shard_map/ppermute | solution.py:323
  73.7 6.4 %collective-permute-start.13 = (f32[2,2,1]{2,1,0:T(2,128)S(1)}, f32[2,2,1]{2,1,0:T(2,128)S(1)}, u32[]{:S(2)}, u32[]{:S(2)}) collective-permute-start(f32[2,2,1]{2,1,0:T(2,128)S(1)} %get-tuple-element.61), channel_id=1, source_target_pairs={{0,8},{1,9},{2,10},{3,11},{12,4},{13,5},{14,6},{15,7},{16,24},{17,... | collective-permute-start | bytes 56 | tf_op jit(solution)/shard_map/ppermute | solution.py:373
